TPU v7x, 256 devices: a whole 4x4x8 slice. The times are simulated.
256 devices in a mesh: prot: 16 (over y, x_hi, core), var: 8 (over z), samp: 2 (over x_lo).
Axes of the slice: x: 4 (x_hi: 2, x_lo: 2; x = x_hi * 2 + x_lo), y: 4, z: 8, core: 2. Of those that a mesh axis runs over, the one named last changes fastest.
Arguments:
- genotype: bfloat16 [196608, 2048], P(('prot', 'var'), 'samp'), may hold values from 0 to 2
- proteins: bfloat16 [2048, 2944], P('samp', 'prot'), may hold values from -16 to 16
- cis_pick: int32 [128, 16], P(('prot', 'var')), may hold values from -1 to 23, as said below
- perm_table: int32 [4, 2048], P(None, 'samp'), may hold values from 0 to 2047, each once within a row
Outputs:
- trans_score: bfloat16 [196608, 2944], P(('prot', 'var'), 'samp')
- cis_stat: float32 [4, 2944], P(None, 'prot')
Inputs may be any that keep to these rules, and one draw needn't show every extreme that they name: `cis_pick`: each entry names one of the 24 cis blocks of its slab, or is -1 for no cis block. `perm_table`: each row holds every sample index once.
All inputs are finite; a program needn't handle non-finite values.
Results may differ from a plain program's by a relative error of at most 0.001.
Values may be sent and summed in bfloat16 or wider, within the bound.
A program may use at most 128 MiB of HBM per device.

v0:
```python
import jax
import jax.numpy as jnp
from jax import lax
from jax.sharding import PartitionSpec as P

VB = 64


epsilon = 1e-06


def finish_trans(cross, col_moments, row_moments, count_all):
    mean_g = row_moments[:, 0] / count_all
    var_g = row_moments[:, 1] / count_all - mean_g * mean_g
    mean_y = col_moments[0] / count_all
    var_y = col_moments[1] / count_all - mean_y * mean_y
    covar = cross / count_all - mean_g[:, None] * mean_y[None, :]
    return (
        jnp.sqrt(count_all)
        * covar
        * lax.rsqrt(var_g + epsilon)[:, None]
        * lax.rsqrt(var_y + epsilon)[None, :]
    )


def trans_part(genotype, proteins):
    samp_count = lax.axis_size("samp")
    local_samples, block_width = proteins.shape
    count_all = jnp.float32(local_samples * samp_count)
    slab_piece = lax.all_gather(proteins, "prot", axis=1, tiled=True)
    product = jnp.dot(genotype, slab_piece, preferred_element_type=jnp.float32)
    widened = slab_piece.astype(jnp.float32)
    piece_moments = jnp.stack([jnp.sum(widened, 0), jnp.sum(widened * widened, 0)])
    col_moments = piece_moments
    cross, col_moments = (product, col_moments)
    row_wide = genotype.astype(jnp.float32)
    row_moments = jnp.stack([jnp.sum(row_wide, 1), jnp.sum(row_wide * row_wide, 1)], 1)
    cross, col_moments = (
        lax.psum_scatter(cross, "samp", scatter_dimension=1, tiled=True),
        lax.psum_scatter(col_moments, "samp", scatter_dimension=1, tiled=True),
    )
    row_moments = lax.psum(row_moments, "samp")
    score = finish_trans(cross, col_moments, row_moments, count_all).astype(jnp.bfloat16)
    return score


def cis_part(genotype, proteins, cis_pick, perm_table):
    samp_count = lax.axis_size("samp")
    prot_count = lax.axis_size("prot")
    var_count = lax.axis_size("var")
    local_samples, block_width = proteins.shape
    count_all = jnp.float32(local_samples * samp_count)
    blocks = genotype.reshape(genotype.shape[0] // VB, VB, local_samples)
    chosen_ids = cis_pick[0]
    keep_mask = (chosen_ids >= 0).astype(jnp.bfloat16)
    chosen = jnp.take(blocks, jnp.maximum(chosen_ids, 0), axis=0) * keep_mask[:, None, None]
    arrived = lax.all_to_all(chosen, "prot", split_axis=0, concat_axis=0, tiled=True)
    cis_rows = arrived.reshape(prot_count * VB, local_samples)
    full_block = lax.all_gather(proteins, "samp", axis=0, tiled=True)
    block_wide = full_block.astype(jnp.float32)
    mean_y = jnp.sum(block_wide, 0) / count_all
    var_y = jnp.sum(block_wide * block_wide, 0) / count_all - mean_y * mean_y
    perm_count = perm_table.shape[0]
    permuted = jnp.take(full_block, perm_table, axis=0)
    stacked = permuted.transpose(1, 0, 2).reshape(local_samples, perm_count * block_width)
    cross = jnp.dot(cis_rows, stacked, preferred_element_type=jnp.float32)
    row_wide = cis_rows.astype(jnp.float32)
    row_moments = jnp.stack([jnp.sum(row_wide, 1), jnp.sum(row_wide * row_wide, 1)], 1)
    cross, row_moments = (
        lax.psum_scatter(cross, "samp", scatter_dimension=0, tiled=True),
        lax.psum_scatter(row_moments, "samp", scatter_dimension=0, tiled=True),
    )
    mean_g = row_moments[:, 0] / count_all
    var_g = row_moments[:, 1] / count_all - mean_g * mean_g
    mean_tiled = jnp.tile(mean_y, perm_count)
    inv_tiled = jnp.tile(lax.rsqrt(var_y + epsilon), perm_count)
    covar = cross / count_all - mean_g[:, None] * mean_tiled[None, :]
    score = jnp.sqrt(count_all) * covar * lax.rsqrt(var_g + epsilon)[:, None] * inv_tiled[None, :]
    column_sums = jnp.sum(score * score, 0).reshape(perm_count, block_width)
    column_sums = column_sums / jnp.float32(VB * prot_count * var_count)
    return lax.psum(column_sums, ("var", "samp"))


def body(genotype, proteins, cis_pick, perm_table):
    trans_score = trans_part(genotype, proteins)
    cis_stat = cis_part(genotype, proteins, cis_pick, perm_table)
    return (trans_score, cis_stat)


def solution(mesh):
    return jax.shard_map(
        body,
        mesh=mesh,
        in_specs=(
            P(("prot", "var"), "samp"),
            P("samp", "prot"),
            P(("prot", "var"), None),
            P(None, "samp"),
        ),
        out_specs=(P(("prot", "var"), "samp"), P(None, "prot")),
        check_vma=False,
    )
```

profile of v0, /device:TPU:1, one launch (start us, length us, event | category | flops | bytes accessed | tf_op | source)
XLA Modules:
  0.0 422.3 jit_solution(9932665872259995)
XLA Ops:
  8.0 0.0 all-gather.2.cloned.1.call-start
  8.0 0.7 all-gather.2.cloned.1.call-update
  8.7 0.7 maximum_bitcast_fusion
  9.4 2.6 gather_fusion
  12.0 1.6 select_multiply_fusion
  13.6 8.6 %all-to-all-start = ((bf16[16,64,1024]{2,1,0:T(8,128)(2,1)}), bf16[16,64,1024]{2,1,0:T(8,128)(2,1)S(1)}, u32[]{:S(2)}, u32[]{:S(2)}) async-start(bf16[16,64,1024]{2,1,0:T(8,128)(2,1)} %select_multiply_fusion), calls=%async_computation.1 | async-start | bytes 4194304 | tf_op jit(solution)/shard_map/all_to_all | solution.py:57
  22.2 0.0 reduce-scatter.15.cloned.1.call-start
  22.3 1.0 copy.9
  23.2 38.8 %all_gather.7 = bf16[2048,184]{1,0:T(8,128)(2,1)S(1)} all-gather(bf16[1024,184]{1,0:T(8,128)(2,1)} %copy.9), channel_id=1, replica_groups=mesh['prot'=16,'var'=8,'samp'=2] {'samp'}, dimensions={0}, use_global_device_ids=true | all-gather | bytes 1130496 | tf_op jit(solution)/shard_map/all_gather | solution.py:59
  62.0 16.9 %gather_fusion.1 = bf16[4096,184]{1,0:T(8,128)(2,1)} fusion(bf16[2048,184]{1,0:T(8,128)(2,1)S(1)} %all_gather.7, s32[4096]{0:T(1024)S(1)} %bitcast_clamp_fusion), kind=kCustom, calls=%fused_computation.1 | custom fusion | bytes 3031040 | tf_op jit(solution)/shard_map/jit(_take)/gather | solution.py:64
  79.0 3.9 copy.10
  82.9 2.7 bitcast_select_fusion
  85.6 0.8 convert_reduce_fusion.2
  86.4 0.1 stack.33
  86.5 0.1 stack.34
  86.6 1.0 copy.13
  87.6 0.0 reduce-scatter.15.cloned.1.call-update
  87.6 0.0 reduce-scatter.11.cloned.1.call-start
  87.7 4.8 %fusion.11 = f32[1024,736]{0,1:T(8,128)} fusion(bf16[1024,1024]{1,0:T(8,128)(2,1)S(1)} %bitcast.28, bf16[1024,736]{0,1:T(8,128)(2,1)} %bitcast.32), kind=kOutput, calls=%fused_computation.45 | convolution fusion | flops 1543503872 | bytes 6619136 | tf_op jit(solution)/shard_map/dot_general | solution.py:66
  92.5 0.0 reduce-scatter.11.cloned.1.call-update
  92.5 0.0 reduce-scatter.13.cloned.1.call-start
  92.5 4.3 %all-gather.2.cloned.1.call-done = bf16[1024,2944]{0,1:T(8,128)(2,1)} async-done(((bf16[1024,184]{0,1:T(8,128)(2,1)}), bf16[1024,2944]{0,1:T(8,128)(2,1)}) %all-gather.2.cloned.1.call-update) | async-done | bytes 6029328 | tf_op jit(solution)/shard_map/all_gather | solution.py:30
  96.8 4.5 %convert_reduce_fusion = (f32[2944]{0:T(1024)S(1)}, f32[2944]{0:T(1024)S(1)}) fusion(bf16[1024,2944]{0,1:T(8,128)(2,1)} %all-gather.2.cloned.1.call-done), kind=kLoop, calls=%fused_computation.3 | loop fusion | flops 12052736 | bytes 6052864 | tf_op jit(solution)/shard_map/reduce_sum | solution.py:33
  101.3 1.7 copy.11
  103.0 0.0 reduce-scatter.13.cloned.1.call-update
  103.1 0.2 reduce-scatter.9.cloned.1.call-start
  103.3 16.1 %fusion.10 = f32[1536,2944]{0,1:T(8,128)} fusion(bf16[1536,1024]{1,0:T(8,128)(2,1)} %param.4, bf16[1024,2944]{0,1:T(8,128)(2,1)} %all-gather.2.cloned.1.call-done), kind=kOutput, calls=%fused_computation.44 | convolution fusion | flops 9261023232 | bytes 27262976 | tf_op jit(solution)/shard_map/dot_general | solution.py:31
  119.5 0.0 reduce-scatter.9.cloned.1.call-update
  119.5 2.8 convert_reduce_fusion.1
  122.4 0.4 convert_reduce_fusion.3
  122.7 0.1 mul.151
  122.8 0.1 mul.162
  122.9 5.3 %psum.14 = f32[1536,2]{0,1:T(2,128)S(1)} all-reduce(f32[1536,2]{0,1:T(2,128)S(1)} %pad_maximum_fusion.1), channel_id=1, replica_groups=mesh['prot'=16,'var'=8,'samp'=2] {'samp'}, use_global_device_ids=true, to_apply=%region_3.0 | all-reduce | flops 3072 | bytes 24576 | tf_op jit(solution)/shard_map/psum | solution.py:42
  128.3 0.0 reduce-scatter.15.cloned.1.call-done
  128.3 1.2 fusion.9
  129.5 0.1 copy.17
  129.6 0.1 copy.18
  129.8 32.6 %reduce-scatter.11.cloned.1.call-done = f32[512,736]{0,1:T(8,128)} async-done(((f32[1024,736]{0,1:T(8,128)}), f32[512,736]{0,1:T(8,128)}) %reduce-scatter.11.cloned.1.call-update) | async-done | bytes 1507344 | tf_op jit(solution)/shard_map/reduce_scatter | solution.py:70
  162.3 1.9 multiply_reduce_fusion
  164.3 0.1 div.58
  164.4 27.9 %psum.15 = f32[4,184]{1,0:T(4,128)} all-reduce(f32[4,184]{1,0:T(4,128)S(1)} %div.58), channel_id=1, replica_groups=mesh['prot'=16,'var'=8,'samp'=2] {'var','samp'}, use_global_device_ids=true, to_apply=%region_14.15 | all-reduce | flops 736 | bytes 5888 | tf_op jit(solution)/shard_map/psum | solution.py:81
  192.2 4.6 %reduce-scatter.13.cloned.1.call-done = f32[1472,2]{1,0:T(8,128)} async-done(((f32[2944,2]{1,0:T(8,128)}), f32[1472,2]{1,0:T(8,128)}) %reduce-scatter.13.cloned.1.call-update) | async-done | bytes 11792
  196.8 1.6 fusion.8
  198.4 0.3 copy.16
  198.7 0.3 copy.15
  198.9 0.1 multiply_reduce_fusion.2
  199.0 209.7 %reduce-scatter.9.cloned.1.call-done = f32[1536,1472]{0,1:T(8,128)} async-done(((f32[1536,2944]{0,1:T(8,128)}), f32[1536,1472]{0,1:T(8,128)}) %reduce-scatter.9.cloned.1.call-update) | async-done | bytes 9043984 | tf_op jit(solution)/shard_map/reduce_scatter | solution.py:39
  408.7 6.0 %multiply_convert_fusion = bf16[1536,1472]{0,1:T(8,128)(2,1)} fusion(f32[1536,1472]{0,1:T(8,128)} %reduce-scatter.9.cloned.1.call-done, f32[1472]{0:T(1024)S(1)} %get-tuple-element.13, f32[1536]{0:T(1024)S(1)} %get-tuple-element.11, f32[1472]{0:T(1024)S(1)} %get-tuple-element.12, f32[1536]{0:T(1024)S(1)} %get-tuple-element.10), kind=kLoop, calls=%fused_computation.5 | loop fusion | flops 13565952 | bytes 13590016 | tf_op jit(solution)/shard_map/convert_element_type | solution.py:43
  (25 shorter events, 0.2 us)
Async XLA Ops:
  8.0 88.8 %all-gather.2.cloned.1.call-start = ((), (), s32[]{:S(2)}) async-start(), calls=%async_computation.5 | async-start | bytes 6406144 | tf_op jit(solution)/shard_map/all_gather | solution.py:30
  9.4 2.6 copy-start.2
  13.6 8.6 %copy-start = (bf16[1024,184]{0,1:T(8,128)(2,1)S(1)}, bf16[1024,184]{0,1:T(8,128)(2,1)}, u32[]{:S(2)}) copy-start(bf16[1024,184]{0,1:T(8,128)(2,1)} %param.5) | copy-start | bytes 1130500
  13.6 72.0 %all-to-all-start = ((bf16[16,64,1024]{2,1,0:T(8,128)(2,1)}), bf16[16,64,1024]{2,1,0:T(8,128)(2,1)S(1)}, u32[]{:S(2)}, u32[]{:S(2)}) async-start(bf16[16,64,1024]{2,1,0:T(8,128)(2,1)} %select_multiply_fusion), calls=%async_computation.1 | async-start | bytes 4194304 | tf_op jit(solution)/shard_map/all_to_all | solution.py:57
  22.2 39.8 %copy-start.1 = (s32[4,1024]{1,0:T(4,128)S(1)}, s32[4,1024]{1,0:T(4,128)}, u32[]{:S(2)}) copy-start(s32[4,1024]{1,0:T(4,128)} %param.7) | copy-start | bytes 49156
  22.2 106.1 %reduce-scatter.15.cloned.1.call-start = ((), (), s32[]{:S(2)}) async-start(), calls=%async_computation.9 | async-start | bytes 786432
  87.6 74.7 %reduce-scatter.11.cloned.1.call-start = ((), (), s32[]{:S(2)}) async-start(), calls=%async_computation.7 | async-start | bytes 4521984 | tf_op jit(solution)/shard_map/reduce_scatter | solution.py:70
  92.5 104.3 %reduce-scatter.13.cloned.1.call-start = ((), (), s32[]{:S(2)}) async-start(), calls=%async_computation.8 | async-start | bytes 2260992
  103.1 305.6 %reduce-scatter.9.cloned.1.call-start = ((), (), s32[]{:S(2)}) async-start(), calls=%async_computation.6 | async-start | bytes 27131904 | tf_op jit(solution)/shard_map/reduce_scatter | solution.py:39
Sparse Core Ops, SparseCore 0:
  11.6 85.1 all-gather.1
Sparse Core Ops, SparseCore 1:
  87.7 23.4 reduce-scatter.14
  114.3 48.0 reduce-scatter.10
  164.7 32.0 reduce-scatter.12
  199.6 209.1 reduce-scatter.8
where the time goes:
time: 423 us; the launch traced here: 422 us
  waiting for transfers between devices  252 us (60%)
  blocking collectives  72 us (17%)
  local copies, waits for them, and re-layouts  31.1 us (7%)
  other arithmetic  21.6 us (5%)
  matrix products  20.9 us (5%)
  between operations  15.9 us (4%)
  starting transfers between devices  8.97 us (2%)
    reduce_scatter x1, waiting for transfers between devices, trans_part(): lax.psum_scatter(cross, 'samp', scatter_dimension=1, tiled=True)  210 us
    all_gather x1, blocking collectives, cis_part(): full_block = lax.all_gather(proteins, 'samp', axis=0, tiled=True)  38.8 us
    reduce_scatter x1, waiting for transfers between devices, cis_part(): lax.psum_scatter(cross, 'samp', scatter_dimension=0, tiled=True)  32.6 us
    psum x1, blocking collectives, cis_part(): return lax.psum(column_sums, ('var', 'samp'))  27.9 us
    gather x2, local copies, waits for them, and re-layouts, cis_part(): permuted = jnp.take(full_block, perm_table, axis=0)  20.8 us
    dot_general x1, matrix products, trans_part(): product = jnp.dot(genotype, slab_piece, preferred_element_type=jnp.float32)  16.1 us
    all_to_all x1, starting transfers between devices, cis_part(): lax.all_to_all(chosen, 'prot', split_axis=0, concat_axis=0, tiled=True)  8.58 us
  transfers between devices with their start and end apart: 6, of which 4 were waited for; matrix products, arithmetic and copies ran while one was open for 16% of the time, Pallas kernels for 0%

commit v1 on v0

v1 whole, which is shorter than its diff:
```python
import functools

import jax
import jax.numpy as jnp
from jax import lax
from jax.experimental import pallas as pl
from jax.experimental.pallas import tpu as pltpu
from jax.sharding import PartitionSpec as P

MESH = pl.DeviceIdType.MESH
VB = 64
BLOCKS = 24
TILES = BLOCKS // 2
ROWS = VB * BLOCKS
HALF = 1024
ALL = 2 * HALF
PB = 184
COLS = 8 * PB
CHUNKS = (4, 4, 4, 4, 4, 2, 2)
STARTS = tuple(sum(CHUNKS[:c]) for c in range(len(CHUNKS)))
CIS_CHUNKS = 2
GROUPS = ((4, 0, 8), (5, 8, 10), (6, 10, 11), (7, 11, 12))
EPS = 1e-6
N = float(ALL)
MIB = 1 << 20
NT = (((1,), (1,)), ((), ()))


def dot_nt(a, b):
    return lax.dot_general(a, b, NT, preferred_element_type=jnp.float32)


def block_order(pick_ref, first, flag, order):
    picks = [pick_ref[0, first + i] for i in range(8)]
    for b in range(BLOCKS):
        hit = jnp.int32(0)
        for pick in picks:
            hit = hit | (pick == b).astype(jnp.int32)
        flag[b] = hit
    at = jnp.int32(0)
    for rank in range(3):
        for b in range(BLOCKS):
            mine, pair = flag[b], flag[b ^ 1]
            here = (mine, (1 - mine) * pair, (1 - mine) * (1 - pair))[rank]
            order[at] = jnp.int32(b)
            at = at + here


def sort_kernel(pick_ref, g_ref, *refs):
    outs, (flag, order, sems) = refs[:-3], refs[-3:]
    block_order(pick_ref, 8 * (1 - lax.axis_index("samp")), flag, order)
    copies = []
    for c, blocks in enumerate(CHUNKS):
        for t in range(blocks):
            r = STARTS[c] + t
            row = pl.multiple_of(order[r] * VB, VB)
            copy = pltpu.make_async_copy(g_ref.at[pl.ds(row, VB)], outs[c].at[pl.ds(t * VB, VB)], sems.at[r])
            copy.start()
            copies.append(copy)
    for copy in copies:
        copy.wait()


def sort_blocks(pick, genotype):
    return pl.pallas_call(
        sort_kernel,
        out_shape=[jax.ShapeDtypeStruct((b * VB, HALF), jnp.bfloat16) for b in CHUNKS],
        in_specs=[pl.BlockSpec(memory_space=pltpu.SMEM), pl.BlockSpec(memory_space=pltpu.HBM)],
        out_specs=[pl.BlockSpec(memory_space=pltpu.VMEM)] * len(CHUNKS),
        scratch_shapes=[
            pltpu.SMEM((BLOCKS,), jnp.int32),
            pltpu.SMEM((BLOCKS + 8,), jnp.int32),
            pltpu.SemaphoreType.DMA((BLOCKS,)),
        ],
        compiler_params=pltpu.CompilerParams(vmem_limit_bytes=8 * MIB),
        name="sort_blocks",
    )(pick, genotype)


PLAN_TILE, PLAN_PLACE, PLAN_BLOCK, PLAN_KEEP, PLAN = 24, 36, 44, 52, 64


def plan_kernel(pick_ref, plan, flag, order, seen):
    first = 8 * lax.axis_index("samp")
    block_order(pick_ref, first, flag, order)
    for t in range(TILES):
        seen[t] = jnp.int32(0)
    done = jnp.int32(0)
    for r in range(BLOCKS):
        b = order[r]
        plan[b] = jnp.int32(r)
        t = b // 2
        before = seen[t]
        seen[t] = before + 1
        plan[PLAN_TILE + done] = t
        done = done + before
    for i in range(8):
        pick = pick_ref[0, first + i]
        keep = (pick >= 0).astype(jnp.int32)
        block = jnp.maximum(pick, 0)
        plan[PLAN_PLACE + i] = plan[block] * keep
        plan[PLAN_BLOCK + i] = block
        plan[PLAN_KEEP + i] = keep


def make_plan(pick):
    smem = pl.BlockSpec(memory_space=pltpu.SMEM)
    return pl.pallas_call(
        plan_kernel,
        out_shape=jax.ShapeDtypeStruct((PLAN,), jnp.int32),
        in_specs=[smem],
        out_specs=smem,
        scratch_shapes=[pltpu.SMEM((n,), jnp.int32) for n in (BLOCKS, BLOCKS + 8, TILES)],
        name="make_plan",
    )(pick)


def protein_kernel(prot, perm_ref, data, perm_out, s_own, s_perm, rp, s1, r1, s2, r2, sa, ra, sb, rb, s3, r3, sd, rd):
    p, z, s = lax.axis_index("prot"), lax.axis_index("var"), lax.axis_index("samp")
    c, xh, y = p % 2, (p // 2) % 2, p // 4
    half, a = y // 2, (y % 2) * 2 + xh
    away = (s + half) % 2
    gap = a - y
    own = (1 - away) * (1 - (gap * gap + 8) // 9)

    def device(y2, x2):
        return y2 * 4 + x2 * 2 + c

    barrier = pltpu.get_barrier_semaphore()

    def signal(dev):
        pl.semaphore_signal(barrier, inc=1, device_id=dev, device_id_type=MESH)

    source = device(2 * s + y // 2, y % 2)

    @pl.when(own == 0)
    def _():
        signal((source, z, s))

    signal((source, z, 1 - s))
    y_peers = [(device((y + d) % 4, xh), z, s) for d in (1, 2, 3)]
    up, down = (p, (z + 1) % 8, s), (p, (z + 7) % 8, s)
    sibling, partner = (p + 1 - 2 * c, z, s), (p, z, 1 - s)
    for dev in (*y_peers, up, down, sibling, partner):
        signal(dev)
    keep_perm = pltpu.make_async_copy(perm_ref, perm_out.at[0], s_own)
    keep_perm.start()
    pl.semaphore_wait(barrier, 9 - own)

    def remote(src, dst, ssem, rsem, dev):
        return pltpu.make_async_remote_copy(
            src_ref=src, dst_ref=dst, send_sem=ssem, recv_sem=rsem, device_id=dev, device_id_type=MESH
        )

    sent = []

    def send(src, dst, ssem, rsem, dev):
        copy = remote(src, dst, ssem, rsem, dev)
        copy.start()
        sent.append(copy)

    def arrived(ref, rsem):
        remote(ref, ref, s_own, rsem, sibling).wait_recv()

    def lanes(z2, far=0):
        return pl.ds(pl.multiple_of(far * HALF + 128 * z2, 128), 128)

    src, dst = prot.at[:, lanes(z)], data.at[a, c, :, lanes(z, away)]
    send(src, dst, s1.at[1], r1.at[away], (device(a, 1 - xh), z, half))
    direct = remote(src, dst, s1.at[0], r1.at[away], (device(a, xh), z, half))

    @pl.when(own == 0)
    def _():
        direct.start()

    @pl.when(own == 1)
    def _():
        pltpu.make_async_copy(src, dst, r1.at[0]).start()

    send(perm_ref, perm_out.at[1], s_perm, rp, partner)

    def near(y2, z2):
        return data.at[y2, c, :, lanes(z2)]

    def near_all(z2):
        return data.at[:, c, :, lanes(z2)]

    def far(z2):
        return data.at[y, c, :, lanes(z2, 1)]

    def far_all(y2):
        return data.at[y2, c, :, pl.ds(HALF, HALF)]

    def ring(t, get, ssem, rsem):
        send(get((z + 8 - t) % 8), get((z + 8 - t) % 8), ssem.at[0, t], rsem.at[0, t], up)
        if t < 3:
            send(get((z + t) % 8), get((z + t) % 8), ssem.at[1, t], rsem.at[1, t], down)

    def ring_wait(t, get, rsem):
        arrived(get((z + 7 - t) % 8), rsem.at[0, t])
        if t < 3:
            arrived(get((z + 1 + t) % 8), rsem.at[1, t])

    arrived(near(y, z), r1.at[0])
    for d in (1, 2, 3):
        send(near(y, z), near(y, z), s2.at[d - 1], r2.at[d - 1], y_peers[d - 1])
    arrived(far(z), r1.at[1])
    ring(0, far, sb, rb)
    for d in (1, 2, 3):
        arrived(near((y + 4 - d) % 4, z), r2.at[d - 1])
    ring(0, near_all, sa, ra)
    for t in range(4):
        ring_wait(t, far, rb)
        if t < 3:
            ring(t + 1, far, sb, rb)

    def share(ref, k):
        send(ref, ref, sd.at[k], rd.at[k], sibling)

    for d in (1, 2, 3):
        send(far_all(y), far_all(y), s3.at[d - 1], r3.at[d - 1], y_peers[d - 1])
    share(near_all(z), 0)
    share(far_all(y), 8)
    for t in range(4):
        ring_wait(t, near_all, ra)
        if t < 3:
            ring(t + 1, near_all, sa, ra)
        share(near_all((z + 7 - t) % 8), 1 + t)
        if t < 3:
            share(near_all((z + 1 + t) % 8), 5 + t)
    for d in (1, 2, 3):
        arrived(far_all((y + 4 - d) % 4), r3.at[d - 1])
        share(far_all((y + 4 - d) % 4), 8 + d)

    def theirs_near(z2, k):
        arrived(data.at[:, 1 - c, :, lanes(z2)], rd.at[k])

    theirs_near(z, 0)
    for t in range(4):
        theirs_near((z + 7 - t) % 8, 1 + t)
        if t < 3:
            theirs_near((z + 1 + t) % 8, 5 + t)
    for d in range(4):
        arrived(data.at[(y + 4 - d) % 4, 1 - c, :, pl.ds(HALF, HALF)], rd.at[8 + d])
    arrived(perm_out.at[1], rp)
    keep_perm.wait()
    for copy in sent:
        copy.wait_send()

    @pl.when(own == 0)
    def _():
        direct.wait_send()


PROT_SPACE = pltpu.HBM


def gather_proteins(prot, perm_table):
    dma = pltpu.SemaphoreType.DMA
    space = pl.BlockSpec(memory_space=PROT_SPACE)
    return pl.pallas_call(
        protein_kernel,
        out_shape=[
            jax.ShapeDtypeStruct((4, 2, PB, ALL), jnp.bfloat16),
            jax.ShapeDtypeStruct((2, 4, HALF), jnp.int32),
        ],
        in_specs=[space, space],
        out_specs=[space, space],
        scratch_shapes=[
            dma, dma, dma, dma((2,)), dma((2,)), dma((3,)), dma((3,)), dma((2, 4)), dma((2, 4)),
            dma((2, 4)), dma((2, 4)), dma((3,)), dma((3,)), dma((12,)), dma((12,)),
        ],
        compiler_params=pltpu.CompilerParams(collective_id=1, has_side_effects=True, vmem_limit_bytes=16 * MIB),
        cost_estimate=pl.CostEstimate(flops=0, bytes_accessed=80 * MIB, transcendentals=0),
        name="gather_proteins",
    )(prot, perm_table)


def moments(a, b):
    a, b = a.astype(jnp.float32), b.astype(jnp.float32)
    mean = (jnp.sum(a, 1, keepdims=True) + jnp.sum(b, 1, keepdims=True)) / N
    var = (jnp.sum(a * a, 1, keepdims=True) + jnp.sum(b * b, 1, keepdims=True)) / N - mean * mean
    return mean, var


def scales(a, b):
    mean, var = moments(a, b)
    inv = jnp.sqrt(jnp.float32(N)) * lax.rsqrt(var + EPS)
    return inv / N, inv * mean


def as_rows(x, y):
    lane = lax.broadcasted_iota(jnp.int32, (x.shape[0], 128), 1)
    turned = jnp.transpose(jnp.where(lane == 0, x, y))
    return turned[0:1, :], turned[1:2, :]


MB = 256


def cis_kernel(plan, samp, perm, prot, g_ref, *refs):
    got = refs[:CIS_CHUNKS]
    out, stat, chosen, moved, sems = refs[CIS_CHUNKS:]
    k, m = pl.program_id(0), pl.program_id(1)

    @pl.when((k == 0) & (m == 0))
    def _():
        copies = []
        for i in range(8):
            row = pl.multiple_of(plan[PLAN_BLOCK + i] * VB, VB)
            copy = pltpu.make_async_copy(
                g_ref.at[pl.ds(row, VB)], chosen.at[pl.ds(i * VB, VB), pl.ds(0, HALF)], sems.at[i]
            )
            copy.start()
            copies.append(copy)
        for i in range(8):
            place = plan[PLAN_PLACE + i]
            for c in range(CIS_CHUNKS):

                @pl.when((place >= STARTS[c]) & (place < STARTS[c] + CHUNKS[c]))
                def _():
                    row = pl.multiple_of((place - STARTS[c]) * VB, VB)
                    chosen[i * VB : (i + 1) * VB, HALF:] = got[c][pl.ds(row, VB), :]

        for i in range(8):
            mean, var = moments(prot[i, :, :HALF], prot[i, :, HALF:])
            stat[0, i] = jnp.broadcast_to(mean, (PB, 128))
            stat[1, i] = jnp.broadcast_to(lax.rsqrt(var + EPS), (PB, 128))
        for copy in copies:
            copy.wait()

    here = lax.broadcasted_iota(jnp.int32, (MB, HALF), 0) + m * MB
    total = jnp.zeros((8 * VB, MB), jnp.float32)
    for side in range(2):
        goal = (perm[side, pl.ds(k, 1), :] + samp[0] * HALF) & (ALL - 1)
        hot = (goal == here).astype(jnp.float32).astype(jnp.bfloat16)
        total += dot_nt(chosen[:, side * HALF : (side + 1) * HALF], hot)
    total = total.astype(jnp.bfloat16)
    at = pl.ds(pl.multiple_of(m * MB, MB), MB)
    for i in range(8):
        moved[i, pl.ds(pl.multiple_of(k * VB, VB), VB), at] = total[i * VB : (i + 1) * VB]

    @pl.when((k == 3) & (m == ALL // MB - 1))
    def _():
        for i in range(8):
            rows = chosen[i * VB : (i + 1) * VB, :]
            by, off = scales(rows[:, :HALF], rows[:, HALF:])
            mean, inv = as_rows(stat[0, i], stat[1, i])
            cross = dot_nt(moved[i], prot[i])
            for j in range(4):
                u = cross[j * VB : (j + 1) * VB] * by - off * mean
                total = jnp.sum(u * u, 0, keepdims=True) * (inv * inv)
                out[i, j : j + 1, :PB] = jnp.where(plan[PLAN_KEEP + i] == 1, total, 0.0)


def cis(plan, samp, perm, prot, genotype, got):
    smem, vmem = pl.BlockSpec(memory_space=pltpu.SMEM), pl.BlockSpec(memory_space=pltpu.VMEM)
    return pl.pallas_call(
        cis_kernel,
        grid=(4, ALL // MB),
        out_shape=[
            jax.ShapeDtypeStruct((8, 4, 256), jnp.float32),
            jax.ShapeDtypeStruct((2, 8, PB, 128), jnp.float32),
        ],
        in_specs=[smem, smem, vmem, vmem, pl.BlockSpec(memory_space=pltpu.HBM), *[vmem] * CIS_CHUNKS],
        out_specs=[vmem, vmem],
        scratch_shapes=[
            pltpu.VMEM((8 * VB, ALL), jnp.bfloat16),
            pltpu.VMEM((8, 4 * VB, ALL), jnp.bfloat16),
            pltpu.SemaphoreType.DMA((8,)),
        ],
        compiler_params=pltpu.CompilerParams(vmem_limit_bytes=40 * MIB),
        cost_estimate=pl.CostEstimate(flops=20_000_000_000, bytes_accessed=20 * MIB, transcendentals=0),
        name="cis",
    )(plan, samp, perm, prot, genotype, *got[:CIS_CHUNKS])


def cis_sum_kernel(part, out, near, every, mine, s1, r1, s2, r2):
    p, z, s = lax.axis_index("prot"), lax.axis_index("var"), lax.axis_index("samp")
    home = 8 * s + z
    same = lax.rem(p + 16 - home, 16)
    is_home = 1 - (same + 15) // 16
    barrier = pltpu.get_barrier_semaphore()

    def signal(dev):
        pl.semaphore_signal(barrier, inc=1, device_id=dev, device_id_type=MESH)

    for d in range(1, 8):
        signal((p, (z + d) % 8, s))
    for d in range(16):
        dev = ((p + d) % 16, p % 8, p // 8)
        if d == 0:

            @pl.when(is_home == 0)
            def _():
                signal(dev)
        else:
            signal(dev)
    pl.semaphore_wait(barrier, 23 - is_home)

    def copy_to(src, dst, ssem, rsem, dev):
        return pltpu.make_async_remote_copy(
            src_ref=src, dst_ref=dst, send_sem=ssem, recv_sem=rsem, device_id=dev, device_id_type=MESH
        )

    sent = []
    for d in range(1, 8):
        z2 = (z + d) % 8
        copy = copy_to(part.at[z2], near.at[d], s1.at[d], r1.at[d], (p, z2, s))
        copy.start()
        sent.append(copy)
    total = part[z]
    for d, copy in enumerate(sent, 1):
        copy.wait_recv()
        total += near[d]
    mine[...] = total
    last = []
    for dz in range(8):
        for ds in range(2):
            dev = (home, (z + dz) % 8, (s + ds) % 2)
            copy = copy_to(mine, every.at[p], s2.at[dz * 2 + ds], r2.at[p], dev)
            if dz == ds == 0:

                @pl.when(is_home == 0)
                def _():
                    copy.start()

                @pl.when(is_home == 1)
                def _():
                    pltpu.make_async_copy(mine, every.at[p], r2.at[p]).start()

                last.append(copy)
            else:
                copy.start()
                sent.append(copy)
    total = jnp.zeros_like(mine)
    for d in range(16):
        copy_to(mine, every.at[d], s2.at[0], r2.at[d], (p, (z + 1) % 8, s)).wait_recv()
        total += every[d]
    out[...] = total
    for copy in sent:
        copy.wait_send()

    @pl.when(is_home == 0)
    def _():
        last[0].wait_send()


def cis_sum(part):
    dma = pltpu.SemaphoreType.DMA
    return pl.pallas_call(
        cis_sum_kernel,
        out_shape=jax.ShapeDtypeStruct((4, 256), jnp.float32),
        in_specs=[pl.BlockSpec(memory_space=pltpu.VMEM)],
        out_specs=pl.BlockSpec(memory_space=pltpu.VMEM),
        scratch_shapes=[
            pltpu.VMEM((8, 4, 256), jnp.float32),
            pltpu.VMEM((16, 4, 256), jnp.float32),
            pltpu.VMEM((4, 256), jnp.float32),
            dma((8,)), dma((8,)), dma((16,)), dma((16,)),
        ],
        compiler_params=pltpu.CompilerParams(collective_id=2, has_side_effects=True),
        cost_estimate=pl.CostEstimate(flops=0, bytes_accessed=16 * MIB, transcendentals=0),
        name="cis_sum",
    )(part)


def trans_kernel(chunks, first, last, aliased, plan, prot, stat, g_ref, *refs):
    got = refs[:chunks]
    out, near, far, stage, s_near, s_far, s_out = refs[chunks + aliased :]
    steps = [(t, min(t + 2, last)) for t in range(first, last, 2)]

    def fetch(n):
        lo, hi = steps[n]
        slot = n % 2
        for t in range(lo, hi):
            tile = plan[PLAN_TILE + t]
            at = (t - lo) * 128
            row = pl.multiple_of(tile * 128, 128)
            pltpu.make_async_copy(
                g_ref.at[pl.ds(row, 128)], near.at[slot, pl.ds(at, 128)], s_near.at[slot, t - lo]
            ).start()
            for h in range(2):
                place = plan[tile * 2 + h]
                for c in range(chunks):

                    @pl.when((place >= STARTS[c]) & (place < STARTS[c] + CHUNKS[c]))
                    def _():
                        row = pl.multiple_of((place - STARTS[c]) * VB, VB)
                        pltpu.make_async_copy(
                            got[c].at[pl.ds(row, VB)],
                            far.at[slot, pl.ds(at + h * VB, VB)],
                            s_far.at[slot, (t - lo) * 2 + h],
                        ).start()

    def fetched(n):
        lo, hi = steps[n]
        slot = n % 2
        for t in range(lo, hi):
            at = (t - lo) * 128
            pltpu.make_async_copy(
                g_ref.at[pl.ds(0, 128)], near.at[slot, pl.ds(at, 128)], s_near.at[slot, t - lo]
            ).wait()
            for h in range(2):
                pltpu.make_async_copy(
                    got[0].at[pl.ds(0, VB)],
                    far.at[slot, pl.ds(at + h * VB, VB)],
                    s_far.at[slot, (t - lo) * 2 + h],
                ).wait()

    def written(n):
        lo, hi = steps[n]
        slot = n % 2
        for t in range(lo, hi):
            pltpu.make_async_copy(
                stage.at[slot, :, pl.ds((t - lo) * 128, 128)], out.at[:, pl.ds(0, 128)], s_out.at[slot, t - lo]
            ).wait()

    fetch(0)
    for n, (lo, hi) in enumerate(steps):
        slot, width = n % 2, (hi - lo) * 128
        if n + 1 < len(steps):
            fetch(n + 1)
        fetched(n)
        a, b = near[slot, :width, :], far[slot, :width, :]
        by, off = as_rows(*scales(a, b))
        if n >= 2:
            written(n - 2)
        for i in range(8):
            at = slice(i * PB, (i + 1) * PB)
            cross = dot_nt(prot[at, :HALF], a) + dot_nt(prot[at, HALF:], b)
            mean, inv = stat[0, i][:, :1], stat[1, i][:, :1]
            stage[slot, at, :width] = ((cross * by - mean * off) * inv).astype(jnp.bfloat16)
        for t in range(lo, hi):
            column = pl.multiple_of(plan[PLAN_TILE + t] * 128, 128)
            pltpu.make_async_copy(
                stage.at[slot, :, pl.ds((t - lo) * 128, 128)], out.at[:, pl.ds(column, 128)], s_out.at[slot, t - lo]
            ).start()
    for n in range(max(len(steps) - 2, 0), len(steps)):
        written(n)


def trans(chunks, first, last, plan, prot, stat, genotype, got, out):
    vmem, hbm = pl.BlockSpec(memory_space=pltpu.VMEM), pl.BlockSpec(memory_space=pltpu.HBM)
    operands = [plan, prot, stat, genotype, *got[:chunks]]
    specs = [pl.BlockSpec(memory_space=pltpu.SMEM), vmem, vmem, *[hbm] * (1 + chunks)]
    aliases = {}
    if out is not None:
        aliases = {len(operands): 0}
        operands.append(out)
        specs.append(hbm)
    wide = min(2, last - first) * 128
    dma = pltpu.SemaphoreType.DMA
    return pl.pallas_call(
        functools.partial(trans_kernel, chunks, first, last, len(aliases)),
        out_shape=jax.ShapeDtypeStruct((COLS, ROWS), jnp.bfloat16),
        in_specs=specs,
        out_specs=hbm,
        scratch_shapes=[
            pltpu.VMEM((2, wide, HALF), jnp.bfloat16),
            pltpu.VMEM((2, wide, HALF), jnp.bfloat16),
            pltpu.VMEM((2, COLS, wide), jnp.bfloat16),
            dma((2, 2)), dma((2, 4)), dma((2, 2)),
        ],
        input_output_aliases=aliases,
        compiler_params=pltpu.CompilerParams(vmem_limit_bytes=24 * MIB),
        cost_estimate=pl.CostEstimate(
            flops=2 * COLS * ALL * 128 * (last - first), bytes_accessed=8 * MIB, transcendentals=0
        ),
        name="trans",
    )(*operands)


def body(genotype, proteins, cis_pick, perm_table):
    samp = lax.axis_index("samp").astype(jnp.int32).reshape(1)
    mine = sort_blocks(cis_pick, genotype)
    got = [lax.ppermute(chunk, "samp", [(0, 1), (1, 0)]) for chunk in mine]
    plan = make_plan(cis_pick)
    data, perm = gather_proteins(proteins.T, perm_table)
    prot = data.reshape(8, PB, ALL)
    part, stat = cis(plan, samp, perm, prot, genotype, got)
    cis_stat = cis_sum(part)[:, :PB] / jnp.float32(8 * HALF)
    out = None
    for chunks, first, last in GROUPS:
        out = trans(chunks, first, last, plan, prot.reshape(COLS, ALL), stat, genotype, got, out)
    return out.T, cis_stat


def solution(mesh):
    return jax.shard_map(
        body,
        mesh=mesh,
        in_specs=(
            P(("prot", "var"), "samp"),
            P("samp", "prot"),
            P(("prot", "var"), None),
            P(None, "samp"),
        ),
        out_specs=(P(("prot", "var"), "samp"), P(None, "prot")),
        check_vma=False,
    )
```

time: 423 us -> 205 us (0.48)
  waiting for transfers between devices: 252 us -> 0.02 us
  Pallas kernels: 0 us -> 174 us
  blocking collectives: 72 us -> 0 us
  other arithmetic: 21.6 us -> 0.6 us
  matrix products: 20.9 us -> 0 us
  between operations: 15.9 us -> 1.06 us
  local copies, waits for them, and re-layouts: 31.1 us -> 20.6 us
    reduce_scatter x2 -> x0, waiting for transfers between devices: 242 us -> none  [the longest x1 210 us: trans_part(): lax.psum_scatter(cross, 'samp', scatter_dimension=1, tiled=True)]
    pallas_call x0 -> x9, Pallas kernels: none -> 174 us  [the longest x1 86.6 us: gather_proteins(): pl.pallas_call(protein_kernel, out_shape=[jax.ShapeDtypeStruct((4, 2, PB,...]
    all_gather x1 -> x0, blocking collectives: 38.8 us -> none  [cis_part(): full_block = lax.all_gather(proteins, 'samp', axis=0, tiled=True)]
    psum x2 -> x0, blocking collectives: 33.2 us -> none  [the longest x1 27.9 us: cis_part(): return lax.psum(column_sums, ('var', 'samp'))]
    gather x3 -> x0, local copies, waits for them, and re-layouts: 23.4 us -> none  [the longest x2 20.8 us: cis_part(): permuted = jnp.take(full_block, perm_table, axis=0)]
    dot_general x2 -> x0, matrix products: 20.9 us -> none  [the longest x1 16.1 us: trans_part(): product = jnp.dot(genotype, slab_piece, preferred_element_type=jnp.float32)]
    unnamed x13 -> x50, local copies, waits for them, and re-layouts: 4.51 us -> 20.6 us
    reduce_sum x5 -> x0, other arithmetic: 10.4 us -> none  [the longest x1 4.46 us: trans_part(): jnp.sum(widened, 0)]
  transfers between devices with their start and end apart: 6 -> 7, of which waited for: 4 -> 0; matrix products, arithmetic and copies ran while one was open for 16% -> 0% of each run, Pallas kernels for 0% -> 80%
where the time goes in v1:
time: 205 us; the launch traced here: 203 us
  Pallas kernels  174 us (85%)
  local copies, waits for them, and re-layouts  20.6 us (10%)
  starting transfers between devices  6.64 us (3%)
    pallas_call x1, Pallas kernels, gather_proteins(): pl.pallas_call(protein_kernel, out_shape=[jax.ShapeDtypeStruct((4, 2, PB,...  86.6 us
    pallas_call x4, Pallas kernels, trans(): pl.pallas_call(functools.partial(trans_kernel, chunks, first, last, len(a...  32 us
    pallas_call x1, Pallas kernels, cis(): pl.pallas_call(cis_kernel, grid=(4, ALL // MB), out_shape=[jax.ShapeDtype...  30.3 us
    unnamed x50, local copies, waits for them, and re-layouts  20.6 us
    pallas_call x1, Pallas kernels, cis_sum(): pl.pallas_call(cis_sum_kernel, out_shape=jax.ShapeDtypeStruct((4, 256), j...  16.5 us
    pallas_call x1, Pallas kernels, sort_blocks(): pl.pallas_call(sort_kernel, out_shape=[jax.ShapeDtypeStruct((b * VB, HALF...  6.76 us
    ppermute x7, starting transfers between devices, body(): got = [lax.ppermute(chunk, 'samp', [(0, 1), (1, 0)]) for chunk in mine]  6.64 us
  transfers between devices with their start and end apart: 7, of which 0 were waited for; matrix products, arithmetic and copies ran while one was open for 0% of the time, Pallas kernels for 80%

profile of v1, /device:TPU:1, one launch (start us, length us, event | category | flops | bytes accessed | tf_op | source)
XLA Modules:
  0.0 202.7 jit_solution(13757146601774650263)
XLA Ops:
  0.6 0.0 copy-start.2
  0.6 1.9 copy-done.2
  2.5 0.7 copy-done.23
  3.2 6.8 %sort_blocks.1 = (bf16[256,1024]{1,0:T(8,128)(2,1)}, bf16[256,1024]{1,0:T(8,128)(2,1)}, bf16[256,1024]{1,0:T(8,128)(2,1)S(1)}, bf16[256,1024]{1,0:T(8,128)(2,1)S...) custom-call(s32[1,16]{1,0:T(1,128)S(1)} %copy-done.23, ...), custom_call_target="tpu_custom_call" | custom-call | tf_op jit(solution)/shard_map/sort_blocks/pallas_call | solution.py:65
  9.9 2.1 %collective-permute-start = (bf16[256,1024]{1,0:T(8,128)(2,1)}, bf16[256,1024]{1,0:T(8,128)(2,1)S(1)}, u32[]{:S(2)}, u32[]{:S(2)}) collective-permute-start(bf16[256,1024]{1,0:T(8,128)(2,1)} %get-tuple-element.15), channel_id=1, source_target_pairs={{0,1},{1,0},{2,3},{3,2},{4,5},{5,4},{6,7},{7,6},{8,9},{9,8},{10,11... | collective-permute-start | bytes 1572872 | tf_op jit(solution)/shard_map/ppermute | solution.py:577
  12.1 0.1 collective-permute-start.1
  12.2 1.4 collective-permute-start.5
  13.5 0.1 collective-permute-start.6
  13.6 1.4 collective-permute-start.2
  15.0 1.6 make_plan.1.plan
  16.7 0.0 copy-start.18
  16.7 1.0 copy-done.18
  17.7 0.7 copy-done.20
  18.4 86.6 %gather_proteins.1 = (bf16[4,2,184,2048]{3,2,1,0:T(8,128)(2,1)S(1)}, s32[2,4,1024]{2,1,0:T(4,128)S(1)}) custom-call(bf16[184,1024]{1,0:T(8,128)(2,1)S(1)} %bitcast.10, s32[4,1024]{1,0:T(4,128)S(1)} %copy-done.20), custom_call_target="tpu_custom_call" | custom-call | bytes 83886080 | tf_op jit(solution)/shard_map/gather_proteins/pallas_call | solution.py:261
  105.0 0.0 copy-start
  105.0 0.0 collective-permute-done.refs_0_
  105.0 0.0 copy-start.7
  105.0 0.1 collective-permute-start.3
  105.1 0.0 collective-permute-done.1.refs_1_
  105.2 0.0 copy-start.10
  105.2 1.5 collective-permute-start.4
  106.6 2.7 %copy-done.3 = bf16[1536,1024]{1,0:T(8,128)(2,1)S(1)} copy-done((bf16[1536,1024]{1,0:T(8,128)(2,1)S(1)}, bf16[1536,1024]{1,0:T(8,128)(2,1)}, u32[]{:S(2)}) %copy-start.3) | copy-done | bytes 3145752
  109.3 0.7 copy-done.21
  109.9 30.3 %cis.1 = (f32[8,4,256]{2,1,0:T(4,128)S(1)}, f32[2,8,184,128]{3,2,1,0:T(8,128)S(1)}) custom-call(s32[64]{0:T(128)S(1)} %copy-done.21, s32[1]{0:T(128)} %bitcast.2.samp, s32[2,4,1024]{2,1,0:T(4,128)S(1)} %get-tuple-element.14.perm, bf16[8,184,2048]{2,1,0:T(8,128)(2,1)S(1)} %bitcast.5, bf16[1536,1024]{1,0:T(8,128)(2,1)S(1)} %copy-done.3, ...), custom_call_target="tpu_custom_call" | custom-call | flops 20000000000 | bytes 20971520 | tf_op jit(solution)/shard_map/cis/pallas_call | solution.py:358
  140.3 0.0 copy-done.7
  140.3 0.6 copy-done.19
  140.9 0.0 collective-permute-done.2.refs_2_
  140.9 0.8 copy-done.13
  141.8 0.0 collective-permute-done.3.refs_3_
  141.8 1.2 copy-done.8
  143.0 1.0 copy-done.11
  144.1 1.0 copy-done.14
  145.1 17.9 %trans.4.refs_5_ = bf16[1472,1536]{1,0:T(8,128)(2,1)} custom-call(s32[64]{0:T(128)S(1)} %copy-done.21, bf16[1472,2048]{1,0:T(8,128)(2,1)S(1)} %bitcast.6, f32[2,8,184,128]{3,2,1,0:T(8,128)S(1)} %get-tuple-element.17.stat, bf16[1536,1024]{1,0:T(8,128)(2,1)S(1)} %copy-done.3, bf16[256,1024]{1,0:T(8,128)(2,1)S(1)} %copy-done.8, ...), custom_call_target="tpu_custom_call" | custom-call | flops 6174015488 | bytes 8388608 | tf_op jit(solution)/shard_map/trans/pallas_call | solution.py:554
  163.0 16.5 %cis_sum.1 = f32[4,256]{1,0:T(4,128)} custom-call(f32[8,4,256]{2,1,0:T(4,128)} %copy-done.19), custom_call_target="tpu_custom_call" | custom-call | bytes 16777216 | tf_op jit(solution)/shard_map/cis_sum/pallas_call | solution.py:451
  179.5 0.0 collective-permute-done.4.refs_4_
  179.6 2.7 %copy-done.1 = bf16[4,2,184,2048]{3,2,1,0:T(8,128)(2,1)S(1)} copy-done((bf16[4,2,184,2048]{3,2,1,0:T(8,128)(2,1)S(1)}, bf16[4,2,184,2048]{3,2,1,0:T(8,128)(2,1)}, u32[]{:S(2)}) %copy-start.1) | copy-done | bytes 6029336
  182.3 1.4 copy-done.6
  183.7 1.0 copy-done.9
  184.7 1.0 copy-done.12
  185.8 1.0 copy-done.15
  186.8 1.0 copy-done.17
  187.8 5.9 %trans.5.refs_6_ = bf16[1472,1536]{1,0:T(8,128)(2,1)} custom-call(s32[64]{0:T(128)S(1)} %copy-done.22, bf16[1472,2048]{1,0:T(8,128)(2,1)S(1)} %bitcast.7, f32[2,8,184,128]{3,2,1,0:T(8,128)S(1)} %copy-done.6, bf16[1536,1024]{1,0:T(8,128)(2,1)S(1)} %copy-done.4, bf16[256,1024]{1,0:T(8,128)(2,1)S(1)} %copy-done.9, ...), custom_call_target="tpu_custom_call", output_to_operand_aliasing={{}: (9, {})} | custom-call | flops 1543503872 | bytes 8388608 | tf_op jit(solution)/shard_map/trans/pallas_call | solution.py:554
  193.8 0.0 collective-permute-done.5.refs_5_
  193.8 3.8 %trans.6.refs_7_ = bf16[1472,1536]{1,0:T(8,128)(2,1)} custom-call(s32[64]{0:T(128)S(1)} %copy-done.22, bf16[1472,2048]{1,0:T(8,128)(2,1)S(1)} %bitcast.8, f32[2,8,184,128]{3,2,1,0:T(8,128)S(1)} %copy-done.6, bf16[1536,1024]{1,0:T(8,128)(2,1)S(1)} %copy-done.4, bf16[256,1024]{1,0:T(8,128)(2,1)S(1)} %copy-done.9, ...), custom_call_target="tpu_custom_call", output_to_operand_aliasing={{}: (10, {})} | custom-call | flops 771751936 | bytes 8388608 | tf_op jit(solution)/shard_map/trans/pallas_call | solution.py:554
  197.6 0.0 copy-done.24
  197.6 0.6 slice_multiply_fusion
  198.2 0.0 collective-permute-done.6.refs_6_
  198.2 4.4 %trans.7 = bf16[1472,1536]{1,0:T(8,128)(2,1)} custom-call(s32[64]{0:T(128)S(1)} %copy-done.22, bf16[1472,2048]{1,0:T(8,128)(2,1)S(1)} %bitcast.9, f32[2,8,184,128]{3,2,1,0:T(8,128)S(1)} %copy-done.6, bf16[1536,1024]{1,0:T(8,128)(2,1)S(1)} %copy-done.4, bf16[256,1024]{1,0:T(8,128)(2,1)S(1)} %copy-done.9, ...), custom_call_target="tpu_custom_call", output_to_operand_aliasing={{}: (11, {})} | custom-call | flops 771751936 | bytes 8388608 | tf_op jit(solution)/shard_map/trans/pallas_call | solution.py:554
  (26 shorter events, 0.0 us)
Async XLA Ops:
  0.6 1.9 copy-start.2
  2.5 0.7 copy-start.23
  9.9 95.1 %collective-permute-start = (bf16[256,1024]{1,0:T(8,128)(2,1)}, bf16[256,1024]{1,0:T(8,128)(2,1)S(1)}, u32[]{:S(2)}, u32[]{:S(2)}) collective-permute-start(bf16[256,1024]{1,0:T(8,128)(2,1)} %get-tuple-element.15), channel_id=1, source_target_pairs={{0,1},{1,0},{2,3},{3,2},{4,5},{5,4},{6,7},{7,6},{8,9},{9,8},{10,11... | collective-permute-start | bytes 1572872 | tf_op jit(solution)/shard_map/ppermute | solution.py:577
  12.1 93.1 %collective-permute-start.1 = (bf16[256,1024]{1,0:T(8,128)(2,1)}, bf16[256,1024]{1,0:T(8,128)(2,1)S(1)}, u32[]{:S(2)}, u32[]{:S(2)}) collective-permute-start(bf16[256,1024]{1,0:T(8,128)(2,1)} %get-tuple-element.16), channel_id=1, source_target_pairs={{0,1},{1,0},{2,3},{3,2},{4,5},{5,4},{6,7},{7,6},{8,9},{9,8},{10,11... | collective-permute-start | bytes 1572872 | tf_op jit(solution)/shard_map/ppermute | solution.py:577
  12.2 181.6 %collective-permute-start.5 = (bf16[128,1024]{1,0:T(8,128)(2,1)}, bf16[128,1024]{1,0:T(8,128)(2,1)S(1)}, u32[]{:S(2)}, u32[]{:S(2)}) collective-permute-start(bf16[128,1024]{1,0:T(8,128)(2,1)} %get-tuple-element.21), channel_id=1, source_target_pairs={{0,1},{1,0},{2,3},{3,2},{4,5},{5,4},{6,7},{7,6},{8,9},{9,8},{10,11... | collective-permute-start | bytes 786440 | tf_op jit(solution)/shard_map/ppermute | solution.py:577
  13.5 184.7 %collective-permute-start.6 = (bf16[128,1024]{1,0:T(8,128)(2,1)}, bf16[128,1024]{1,0:T(8,128)(2,1)}, u32[]{:S(2)}, u32[]{:S(2)}) collective-permute-start(bf16[128,1024]{1,0:T(8,128)(2,1)} %get-tuple-element.22), channel_id=1, source_target_pairs={{0,1},{1,0},{2,3},{3,2},{4,5},{5,4},{6,7},{7,6},{8,9},{9,8},{10,11... | collective-permute-start | bytes 786440 | tf_op jit(solution)/shard_map/ppermute | solution.py:577
  13.6 127.3 %collective-permute-start.2 = (bf16[256,1024]{1,0:T(8,128)(2,1)S(1)}, bf16[256,1024]{1,0:T(8,128)(2,1)S(1)}, u32[]{:S(2)}, u32[]{:S(2)}) collective-permute-start(bf16[256,1024]{1,0:T(8,128)(2,1)S(1)} %get-tuple-element.18), channel_id=1, source_target_pairs={{0,1},{1,0},{2,3},{3,2},{4,5},{5,4},{6,7},{7,6},{8,9},{9,8},{10,11... | collective-permute-start | bytes 1572872 | tf_op jit(solution)/shard_map/ppermute | solution.py:577
  16.7 1.0 copy-start.18
  17.7 0.7 copy-start.20
  105.0 36.8 %copy-start = (bf16[4,2,184,2048]{3,2,1,0:T(8,128)(2,1)}, bf16[4,2,184,2048]{3,2,1,0:T(8,128)(2,1)S(1)}, u32[]{:S(2)}) copy-start(bf16[4,2,184,2048]{3,2,1,0:T(8,128)(2,1)S(1)} %get-tuple-element.13) | copy-start | bytes 18087940
  105.0 35.3 %copy-start.7 = (bf16[256,1024]{1,0:T(8,128)(2,1)}, bf16[256,1024]{1,0:T(8,128)(2,1)S(1)}, u32[]{:S(2)}) copy-start(bf16[256,1024]{1,0:T(8,128)(2,1)S(1)} %collective-permute-done.refs_0_) | copy-start | bytes 1572868
  105.0 36.7 %collective-permute-start.3 = (bf16[256,1024]{1,0:T(8,128)(2,1)S(1)}, bf16[256,1024]{1,0:T(8,128)(2,1)S(1)}, u32[]{:S(2)}, u32[]{:S(2)}) collective-permute-start(bf16[256,1024]{1,0:T(8,128)(2,1)S(1)} %get-tuple-element.19), channel_id=1, source_target_pairs={{0,1},{1,0},{2,3},{3,2},{4,5},{5,4},{6,7},{7,6},{8,9},{9,8},{10,11... | collective-permute-start | bytes 1572872 | tf_op jit(solution)/shard_map/ppermute | solution.py:577
  105.2 35.2 %copy-start.10 = (bf16[256,1024]{1,0:T(8,128)(2,1)}, bf16[256,1024]{1,0:T(8,128)(2,1)S(1)}, u32[]{:S(2)}) copy-start(bf16[256,1024]{1,0:T(8,128)(2,1)S(1)} %collective-permute-done.1.refs_1_) | copy-start | bytes 1572868
  105.2 74.4 %collective-permute-start.4 = (bf16[256,1024]{1,0:T(8,128)(2,1)}, bf16[256,1024]{1,0:T(8,128)(2,1)}, u32[]{:S(2)}, u32[]{:S(2)}) collective-permute-start(bf16[256,1024]{1,0:T(8,128)(2,1)} %get-tuple-element.20), channel_id=1, source_target_pairs={{0,1},{1,0},{2,3},{3,2},{4,5},{5,4},{6,7},{7,6},{8,9},{9,8},{10,11... | collective-permute-start | bytes 1572872 | tf_op jit(solution)/shard_map/ppermute | solution.py:577
  106.6 2.7 %copy-start.3 = (bf16[1536,1024]{1,0:T(8,128)(2,1)S(1)}, bf16[1536,1024]{1,0:T(8,128)(2,1)}, u32[]{:S(2)}) copy-start(bf16[1536,1024]{1,0:T(8,128)(2,1)} %g_ref.11) | copy-start | bytes 9437188
  109.3 0.7 copy-start.21
  140.3 0.6 copy-start.19
  140.9 22.1 %copy-start.5 = (f32[2,8,184,128]{3,2,1,0:T(8,128)}, f32[2,8,184,128]{3,2,1,0:T(8,128)S(1)}, u32[]{:S(2)}) copy-start(f32[2,8,184,128]{3,2,1,0:T(8,128)S(1)} %get-tuple-element.17.stat) | copy-start | bytes 4521988
  140.9 0.8 copy-start.13
  141.8 21.2 %copy-start.16 = (bf16[256,1024]{1,0:T(8,128)(2,1)}, bf16[256,1024]{1,0:T(8,128)(2,1)S(1)}, u32[]{:S(2)}) copy-start(bf16[256,1024]{1,0:T(8,128)(2,1)S(1)} %collective-permute-done.3.refs_3_) | copy-start | bytes 1572868
  141.8 1.2 copy-start.8
  143.0 1.0 copy-start.11
  144.0 1.0 copy-start.14
  145.1 34.5 %copy-start.4 = (bf16[1536,1024]{1,0:T(8,128)(2,1)S(1)}, bf16[1536,1024]{1,0:T(8,128)(2,1)}, u32[]{:S(2)}) copy-start(bf16[1536,1024]{1,0:T(8,128)(2,1)} %g_ref.11) | copy-start | bytes 9437188
  145.1 34.5 %copy-start.22 = (s32[64]{0:T(128)S(1)}, s32[64]{0:T(128)}, u32[]{:S(2)}) copy-start(s32[64]{0:T(128)} %make_plan.1.plan) | copy-start | bytes 772
  179.6 2.7 %copy-start.1 = (bf16[4,2,184,2048]{3,2,1,0:T(8,128)(2,1)S(1)}, bf16[4,2,184,2048]{3,2,1,0:T(8,128)(2,1)}, u32[]{:S(2)}) copy-start(bf16[4,2,184,2048]{3,2,1,0:T(8,128)(2,1)} %copy-done) | copy-start | bytes 18087940
  182.3 1.4 copy-start.6
  183.7 1.0 copy-start.9
  184.7 1.0 copy-start.12
  185.8 1.0 copy-start.15
  186.8 1.0 copy-start.17
  193.8 3.8 %copy-start.24 = (f32[4,256]{1,0:T(4,128)S(1)}, f32[4,256]{1,0:T(4,128)}, u32[]{:S(2)}) copy-start(f32[4,256]{1,0:T(4,128)} %cis_sum.1) | copy-start | bytes 12292

commit v2 on v0

v2 whole, which is shorter than its diff:
```python
import functools

import jax
import jax.numpy as jnp
from jax import lax
from jax.experimental import pallas as pl
from jax.experimental.pallas import tpu as pltpu
from jax.sharding import PartitionSpec as P

MESH = pl.DeviceIdType.MESH
VB = 64
BLOCKS = 24
TILES = BLOCKS // 2
ROWS = VB * BLOCKS
HALF = 1024
ALL = 2 * HALF
PB = 184
COLS = 8 * PB
CHUNKS = (8, 8, 4, 4)
STARTS = tuple(sum(CHUNKS[:c]) for c in range(len(CHUNKS)))
GROUPS = ((2, 0, 8), (3, 8, 10), (4, 10, 12))
EPS = 1e-6
N = float(ALL)
MIB = 1 << 20
NT = (((1,), (1,)), ((), ()))


def dot_nt(a, b):
    return lax.dot_general(a, b, NT, preferred_element_type=jnp.float32)


PLAN_TILE, PLAN_PLACE, PLAN_KEEP, PLAN = 24, 36, 44, 64


def block_order(pick_ref, first, flag, order):
    for b in range(BLOCKS):
        flag[b] = jnp.int32(0)
    for i in range(8):
        flag[pick_ref[0, first + i] & 31] = jnp.int32(1)
    flags = [flag[b] for b in range(BLOCKS)]
    at = jnp.int32(0)
    for rank in range(3):
        for b in range(BLOCKS):
            mine, pair = flags[b], flags[b ^ 1]
            order[at] = jnp.int32(b)
            at = at + (mine, (1 - mine) & pair, (1 - mine) & (1 - pair))[rank]


def sort_kernel(pick_ref, g_ref, *refs):
    outs, (chosen, plan, flag, order, seen) = refs[: len(CHUNKS)], refs[len(CHUNKS) :]
    samp = lax.axis_index("samp")
    block_order(pick_ref, 8 * (1 - samp), flag, order)
    for c, blocks in enumerate(CHUNKS):
        for t in range(blocks):
            row = pl.multiple_of(order[STARTS[c] + t] * VB, VB)
            outs[c][t * VB : (t + 1) * VB, :] = g_ref[pl.ds(row, VB), :]

    block_order(pick_ref, 8 * samp, flag, order)
    for t in range(TILES):
        seen[t] = jnp.int32(0)
    done = jnp.int32(0)
    for r in range(BLOCKS):
        b = order[r]
        plan[b] = jnp.int32(r)
        t = lax.shift_right_logical(b, 1)
        before = seen[t]
        seen[t] = before + 1
        plan[PLAN_TILE + done] = t
        done = done + before
    for i in range(8):
        pick = pick_ref[0, 8 * samp + i]
        keep = (pick >= 0).astype(jnp.int32)
        block = jnp.maximum(pick, 0)
        plan[PLAN_PLACE + i] = plan[block] * keep
        plan[PLAN_KEEP + i] = keep
        chosen[i * VB : (i + 1) * VB, :] = g_ref[pl.ds(pl.multiple_of(block * VB, VB), VB), :]


def sort_blocks(pick, genotype):
    smem, vmem = pl.BlockSpec(memory_space=pltpu.SMEM), pl.BlockSpec(memory_space=pltpu.VMEM)
    *mine, chosen, plan = pl.pallas_call(
        sort_kernel,
        out_shape=[
            *[jax.ShapeDtypeStruct((b * VB, HALF), jnp.bfloat16) for b in CHUNKS],
            jax.ShapeDtypeStruct((8 * VB, HALF), jnp.bfloat16),
            jax.ShapeDtypeStruct((PLAN,), jnp.int32),
        ],
        in_specs=[smem, vmem],
        out_specs=[vmem] * (len(CHUNKS) + 1) + [smem],
        scratch_shapes=[pltpu.SMEM((n,), jnp.int32) for n in (32, 32, TILES)],
        compiler_params=pltpu.CompilerParams(vmem_limit_bytes=14 * MIB),
        name="sort_blocks",
    )(pick, genotype)
    return mine, chosen, plan


def choose_kernel(plan, got, chosen):
    for i in range(8):
        row = pl.multiple_of(plan[PLAN_PLACE + i] * VB, VB)
        chosen[i * VB : (i + 1) * VB, :] = got[pl.ds(row, VB), :]


def choose(plan, got):
    vmem = pl.BlockSpec(memory_space=pltpu.VMEM)
    return pl.pallas_call(
        choose_kernel,
        out_shape=jax.ShapeDtypeStruct((8 * VB, HALF), jnp.bfloat16),
        in_specs=[pl.BlockSpec(memory_space=pltpu.SMEM), vmem],
        out_specs=vmem,
        compiler_params=pltpu.CompilerParams(vmem_limit_bytes=4 * MIB),
        name="choose",
    )(plan, got)


MB = 256


def move_step(m, goals, chosen, store):
    here = lax.broadcasted_iota(jnp.int32, (MB, HALF), 0) + m * MB
    at = pl.ds(pl.multiple_of(m * MB, MB), MB)
    for k in range(4):
        hot = jnp.where(goals[k : k + 1, :] == here, 1.0, 0.0).astype(jnp.bfloat16)
        total = dot_nt(chosen[...], hot).astype(jnp.bfloat16)
        for i in range(8):
            store((i, slice(k * VB, (k + 1) * VB), at), total[i * VB : (i + 1) * VB])


def protein_kernel(prot, perm, chosen, data, moved, goals, s_own, s1, r1, s2, r2, sa, ra, sb, rb, s3, r3, sd, rd):
    p, z, s = lax.axis_index("prot"), lax.axis_index("var"), lax.axis_index("samp")
    c, xh, y = p % 2, (p // 2) % 2, p // 4
    half, a = y // 2, (y % 2) * 2 + xh
    away = (s + half) % 2

    def device(y2, x2):
        return y2 * 4 + x2 * 2 + c

    barrier = pltpu.get_barrier_semaphore()

    def signal(dev):
        pl.semaphore_signal(barrier, inc=1, device_id=dev, device_id_type=MESH)

    source = device(2 * s + y // 2, y % 2)
    y_peers = [(device((y + d) % 4, xh), z, s) for d in (1, 2, 3)]
    up, down = (p, (z + 1) % 8, s), (p, (z + 7) % 8, s)
    sibling = (p + 1 - 2 * c, z, s)
    for dev in ((source, (z + 7) % 8, s), (source, (z + 7) % 8, 1 - s), *y_peers, up, down, sibling):
        signal(dev)
    goals[...] = (perm[...] + s * HALF) & (ALL - 1)
    pl.semaphore_wait(barrier, 8)

    def remote(src, dst, ssem, rsem, dev):
        return pltpu.make_async_remote_copy(
            src_ref=src, dst_ref=dst, send_sem=ssem, recv_sem=rsem, device_id=dev, device_id_type=MESH
        )

    def send(src, dst, ssem, rsem, dev):
        remote(src, dst, ssem, rsem, dev).start()

    def arrived(ref, rsem):
        remote(ref, ref, s_own, rsem, sibling).wait_recv()

    def left(ref, ssem):
        remote(ref, ref, ssem, s_own, sibling).wait_send()

    def lanes(z2, far=0):
        return pl.ds(pl.multiple_of(far * HALF + 128 * z2, 128), 128)

    def near(y2, z2):
        return data.at[y2, c, :, lanes(z2)]

    def near_all(z2):
        return data.at[:, c, :, lanes(z2)]

    def far(y2, z2):
        return data.at[y2, c, :, lanes(z2, 1)]

    def far_all(y2):
        return data.at[y2, c, :, pl.ds(HALF, HALF)]

    def pass_near(t, k, downward=True):
        y2 = (y + 4 - k) % 4
        here = near(y2, (z + 8 - t) % 8)
        send(here, here, sa.at[0, t, k], ra.at[0, t, k], up)

        @pl.when(t < 3)
        def _():
            here = near(y2, (z + t) % 8)
            send(here, here, sa.at[1, t, k], ra.at[1, t, k], down)

    def pass_far(t):
        here = far(y, (z + 8 - t) % 8)
        send(here, here, sb.at[0, t], rb.at[0, t], up)

        @pl.when(t < 3)
        def _():
            here = far(y, (z + t) % 8)
            send(here, here, sb.at[1, t], rb.at[1, t], down)

    def spread_far(dz):
        here = far(y, (z + dz) % 8)
        for d in (1, 2, 3):
            send(here, here, s3.at[d - 1, dz], r3.at[d - 1, dz], y_peers[d - 1])

    def share(ref, k):
        send(ref, ref, sd.at[k], rd.at[k], sibling)

    def ring(t):
        arrived(far(y, (z + 7 - t) % 8), rb.at[0, t])

        @pl.when(t < 3)
        def _():
            arrived(far(y, (z + 1 + t) % 8), rb.at[1, t])
            pass_far(t + 1)
            spread_far(1 + t)

        spread_far(7 - t)
        for k in range(4):
            y2 = (y + 4 - k) % 4
            arrived(near(y2, (z + 7 - t) % 8), ra.at[0, t, k])

            @pl.when(t < 3)
            def _():
                arrived(near(y2, (z + 1 + t) % 8), ra.at[1, t, k])
                pass_near(t + 1, k)

        share(near_all((z + 7 - t) % 8), 1 + t)

        @pl.when(t < 3)
        def _():
            share(near_all((z + 1 + t) % 8), 5 + t)

    def step(n, _):
        @pl.when(n == 0)
        def _():
            z2 = (z + 1) % 8
            src, dst = prot.at[:, lanes(z2)], data.at[a, c, :, lanes(z2, away)]
            for x2 in range(2):
                send(src, dst, s1.at[x2], r1.at[away], (device(a, x2), z2, half))

        @pl.when(n == 1)
        def _():
            arrived(near(y, z), r1.at[0])
            for d in (1, 2, 3):
                send(near(y, z), near(y, z), s2.at[d - 1], r2.at[d - 1], y_peers[d - 1])
            pass_near(0, 0)
            arrived(far(y, z), r1.at[1])
            pass_far(0)
            spread_far(0)

        @pl.when(n == 2)
        def _():
            for d in (1, 2, 3):
                arrived(near((y + 4 - d) % 4, z), r2.at[d - 1])
                pass_near(0, d)
            share(near_all(z), 0)

        @pl.when((n >= 2) & (n < 6))
        def _():
            ring(n - 2)

        move_step(n, goals, chosen, lambda at, value: moved.__setitem__(at, value))
        return 0

    lax.fori_loop(0, ALL // MB, step, 0)
    share(far_all(y), 8)
    for d in (1, 2, 3):
        for dz in range(8):
            arrived(far((y + 4 - d) % 4, (z + dz) % 8), r3.at[d - 1, dz])
        share(far_all((y + 4 - d) % 4), 8 + d)

    def theirs_near(z2, k):
        arrived(data.at[:, 1 - c, :, lanes(z2)], rd.at[k])

    theirs_near(z, 0)
    for t in range(4):
        theirs_near((z + 7 - t) % 8, 1 + t)
        if t < 3:
            theirs_near((z + 1 + t) % 8, 5 + t)
    for d in range(4):
        arrived(data.at[(y + 4 - d) % 4, 1 - c, :, pl.ds(HALF, HALF)], rd.at[8 + d])

    one = near(y, z)
    for x2 in range(2):
        left(one, s1.at[x2])
    for d in range(3):
        left(one, s2.at[d])
        for dz in range(8):
            left(one, s3.at[d, dz])
    for t in range(4):
        for way in range(2 if t < 3 else 1):
            left(one, sb.at[way, t])
            for k in range(4):
                left(one, sa.at[way, t, k])
    for k in range(8):
        left(near_all(z), sd.at[k])
    for k in range(8, 12):
        left(far_all(y), sd.at[k])


def gather_proteins(prot, perm, chosen):
    dma = pltpu.SemaphoreType.DMA
    space, vmem = pl.BlockSpec(memory_space=pl.ANY), pl.BlockSpec(memory_space=pltpu.VMEM)
    return pl.pallas_call(
        protein_kernel,
        out_shape=[
            jax.ShapeDtypeStruct((4, 2, PB, ALL), jnp.bfloat16),
            jax.ShapeDtypeStruct((8, 4 * VB, ALL), jnp.bfloat16),
        ],
        in_specs=[space, vmem, vmem],
        out_specs=[space, vmem],
        scratch_shapes=[
            pltpu.VMEM((4, HALF), jnp.int32),
            dma, dma((2,)), dma((2,)), dma((3,)), dma((3,)), dma((2, 4, 4)), dma((2, 4, 4)),
            dma((2, 4)), dma((2, 4)), dma((3, 8)), dma((3, 8)), dma((12,)), dma((12,)),
        ],
        compiler_params=pltpu.CompilerParams(collective_id=1, has_side_effects=True, vmem_limit_bytes=24 * MIB),
        cost_estimate=pl.CostEstimate(flops=9_000_000_000, bytes_accessed=80 * MIB, transcendentals=0),
        name="gather_proteins",
    )(prot, perm, chosen)


def moments(a, b):
    a, b = a.astype(jnp.float32), b.astype(jnp.float32)
    mean = (jnp.sum(a, 1, keepdims=True) + jnp.sum(b, 1, keepdims=True)) / N
    var = (jnp.sum(a * a, 1, keepdims=True) + jnp.sum(b * b, 1, keepdims=True)) / N - mean * mean
    return mean, var


def scales(a, b):
    mean, var = moments(a, b)
    inv = jnp.sqrt(jnp.float32(N)) * lax.rsqrt(var + EPS)
    return inv / N, inv * mean


def as_rows(x, y):
    lane = lax.broadcasted_iota(jnp.int32, (x.shape[0], 128), 1)
    turned = jnp.transpose(jnp.where(lane == 0, x, y))
    return turned[0:1, :], turned[1:2, :]


def cis_kernel(plan, perm, prot, chosen_own, chosen, moved_own, out, stat, goals, moved, part, sums, near, every, s1, r1, s2, r2):
    p, z, s = lax.axis_index("prot"), lax.axis_index("var"), lax.axis_index("samp")
    barrier = pltpu.get_barrier_semaphore()

    def signal(dev):
        pl.semaphore_signal(barrier, inc=1, device_id=dev, device_id_type=MESH)

    for d in range(1, 8):
        signal((p, (z + d) % 8, s))
    home = p % 8
    at_home = 1 - ((z - home) * (z - home) + 63) // 64
    for d in range(16):
        signal((d, (home + at_home) % 8, p // 8))

    goals[...] = (perm[...] + s * HALF) & (ALL - 1)

    def store(at, value):
        moved[at] = moved_own[at] + value

    def move(m, _):
        move_step(m, goals, chosen, store)
        return 0

    lax.fori_loop(0, ALL // MB, move, 0)
    pl.semaphore_wait(barrier, 23)

    def remote(src, dst, ssem, rsem, dev):
        return pltpu.make_async_remote_copy(
            src_ref=src, dst_ref=dst, send_sem=ssem, recv_sem=rsem, device_id=dev, device_id_type=MESH
        )

    def block(n, _):
        i = (z + 1 + n) % 8
        mean, var = moments(prot[i, :, :HALF], prot[i, :, HALF:])
        inv = lax.rsqrt(var + EPS)
        stat[0, i] = jnp.broadcast_to(mean, (PB, 128))
        stat[1, i] = jnp.broadcast_to(inv, (PB, 128))
        mean, inv = as_rows(mean, inv)
        rows = pl.ds(pl.multiple_of(i * VB, VB), VB)
        by, off = scales(chosen_own[rows, :], chosen[rows, :])
        cross = dot_nt(moved[i], prot[i])
        keep = plan[PLAN_KEEP + i].astype(jnp.float32)
        for k in range(4):
            u = cross[k * VB : (k + 1) * VB] * by - off * mean
            part[i, k : k + 1, :PB] = jnp.sum(u * u, 0, keepdims=True) * (inv * inv) * keep

        @pl.when(n != 7)
        def _():
            remote(part.at[i], near.at[0, n], s1.at[0, n], r1.at[0, n], (p, i, s)).start()

        @pl.when(n != 6)
        def _():
            remote(part.at[i], near.at[1, n], s1.at[1, n], r1.at[1, n], (p, (i + 1) % 8, s)).start()

        return 0

    part[...] = jnp.zeros_like(part)
    lax.fori_loop(0, 8, block, 0)

    own_sends = []
    for side in range(2):
        total = part[(z + 8 - side) % 8]
        for n in range(8):
            if n != 7 - side:
                remote(part.at[0], near.at[side, n], s1.at[side, n], r1.at[side, n], (p, (z + 1) % 8, s)).wait_recv()
                total += near[side, n]
        sums[side] = total
        for ds in range(2):
            for dz in range(1, 8) if side == 0 else (7,):
                to = (8 * s + (z + 8 - side) % 8, (z + dz) % 8, (s + ds) % 2)
                copy = remote(sums.at[side], every.at[p], s2.at[side, ds, dz], r2.at[p], to)
                copy.start()
                own_sends.append(copy)
    total = jnp.zeros((4, 256), jnp.float32)
    for d in range(16):
        remote(sums.at[0], every.at[d], s2.at[0, 0, 0], r2.at[d], (p, (z + 1) % 8, s)).wait_recv()
        total += every[d]
    out[...] = total
    for copy in own_sends:
        copy.wait_send()
    for side in range(2):
        for n in range(8):
            if n != 7 - side:
                remote(part.at[0], near.at[side, n], s1.at[side, n], r1.at[side, n], (p, (z + 1) % 8, s)).wait_send()


def cis(plan, perm, prot, chosen_own, chosen_got, moved):
    smem, vmem = pl.BlockSpec(memory_space=pltpu.SMEM), pl.BlockSpec(memory_space=pltpu.VMEM)
    dma = pltpu.SemaphoreType.DMA
    return pl.pallas_call(
        cis_kernel,
        out_shape=[
            jax.ShapeDtypeStruct((4, 256), jnp.float32),
            jax.ShapeDtypeStruct((2, 8, PB, 128), jnp.float32),
        ],
        in_specs=[smem, *[vmem] * 5],
        out_specs=[vmem, vmem],
        scratch_shapes=[
            pltpu.VMEM((4, HALF), jnp.int32),
            pltpu.VMEM((8, 4 * VB, ALL), jnp.bfloat16),
            pltpu.VMEM((8, 4, 256), jnp.float32),
            pltpu.VMEM((2, 4, 256), jnp.float32),
            pltpu.VMEM((2, 8, 4, 256), jnp.float32),
            pltpu.VMEM((16, 4, 256), jnp.float32),
            dma((2, 8)), dma((2, 8)), dma((2, 2, 8)), dma((16,)),
        ],
        compiler_params=pltpu.CompilerParams(collective_id=2, has_side_effects=True, vmem_limit_bytes=36 * MIB),
        cost_estimate=pl.CostEstimate(flops=12_000_000_000, bytes_accessed=20 * MIB, transcendentals=0),
        name="cis",
    )(plan, perm, prot, chosen_own, chosen_got, moved)


def trans_kernel(chunks, first, last, aliased, plan, prot, stat, g_ref, *refs):
    got = refs[:chunks]
    out, rows, stage, sems = refs[chunks + aliased :]
    steps = (last - first) // 2

    def copy_out(n, h):
        column = pl.multiple_of(plan[PLAN_TILE + first + 2 * n + h] * 128, 128)
        return pltpu.make_async_copy(
            stage.at[n % 2, :, pl.ds(h * 128, 128)], out.at[:, pl.ds(column, 128)], sems.at[n % 2, h]
        )

    def step(n, _):
        for t in range(2):
            tile = plan[PLAN_TILE + first + 2 * n + t]
            at = t * 128
            rows[at : at + 128, :HALF] = g_ref[pl.ds(pl.multiple_of(tile * 128, 128), 128), :]
            for h in range(2):
                place = plan[tile * 2 + h]
                for c in range(chunks):

                    @pl.when((place >= STARTS[c]) & (place < STARTS[c] + CHUNKS[c]))
                    def _():
                        row = pl.multiple_of((place - STARTS[c]) * VB, VB)
                        rows[at + h * VB : at + (h + 1) * VB, HALF:] = got[c][pl.ds(row, VB), :]

        both = rows[...]
        by, off = as_rows(*scales(both[:, :HALF], both[:, HALF:]))
        cross = dot_nt(prot[...], both)
        mean = jnp.concatenate([stat[0], stat[0]], 1)
        inv = jnp.concatenate([stat[1], stat[1]], 1)

        @pl.when(n >= 2)
        def _():
            for h in range(2):
                copy_out(n - 2, h).wait()

        stage[n % 2] = ((cross * by - mean * off) * inv).astype(jnp.bfloat16)
        for h in range(2):
            copy_out(n, h).start()
        return 0

    lax.fori_loop(0, steps, step, 0)
    for n in range(max(steps - 2, 0), steps):
        for h in range(2):
            copy_out(n, h).wait()


def trans(chunks, first, last, plan, prot, stat, genotype, got, out):
    vmem, hbm = pl.BlockSpec(memory_space=pltpu.VMEM), pl.BlockSpec(memory_space=pltpu.HBM)
    operands = [plan, prot, stat, genotype, *got[:chunks]]
    specs = [pl.BlockSpec(memory_space=pltpu.SMEM), *[vmem] * (3 + chunks)]
    aliases = {}
    if out is not None:
        aliases = {len(operands): 0}
        operands.append(out)
        specs.append(hbm)
    return pl.pallas_call(
        functools.partial(trans_kernel, chunks, first, last, len(aliases)),
        out_shape=jax.ShapeDtypeStruct((COLS, ROWS), jnp.bfloat16),
        in_specs=specs,
        out_specs=hbm,
        scratch_shapes=[
            pltpu.VMEM((256, ALL), jnp.bfloat16),
            pltpu.VMEM((2, COLS, 256), jnp.bfloat16),
            pltpu.SemaphoreType.DMA((2, 2)),
        ],
        input_output_aliases=aliases,
        compiler_params=pltpu.CompilerParams(vmem_limit_bytes=24 * MIB),
        cost_estimate=pl.CostEstimate(
            flops=2 * COLS * ALL * 128 * (last - first), bytes_accessed=8 * MIB, transcendentals=0
        ),
        name="trans",
    )(*operands)


SWAP = [(0, 1), (1, 0)]


def body(genotype, proteins, cis_pick, perm_table):
    perm_got = lax.ppermute(perm_table, "samp", SWAP)
    mine, chosen, plan = sort_blocks(cis_pick, genotype)
    got = [lax.ppermute(chunk, "samp", SWAP) for chunk in mine]
    data, moved = gather_proteins(proteins.T, perm_table, chosen)
    prot = data.reshape(8, PB, ALL)
    total, stat = cis(plan, perm_got, prot, chosen, choose(plan, got[0]), moved)
    cis_stat = total[:, :PB] / jnp.float32(8 * HALF)
    out = None
    for chunks, first, last in GROUPS:
        out = trans(chunks, first, last, plan, prot.reshape(COLS, ALL), stat.reshape(2, COLS, 128), genotype, got, out)
    return out.T, cis_stat


def solution(mesh):
    return jax.shard_map(
        body,
        mesh=mesh,
        in_specs=(
            P(("prot", "var"), "samp"),
            P("samp", "prot"),
            P(("prot", "var"), None),
            P(None, "samp"),
        ),
        out_specs=(P(("prot", "var"), "samp"), P(None, "prot")),
        check_vma=False,
    )
```

time: 423 us -> 105 us (0.25)
  waiting for transfers between devices: 252 us -> 0.01 us
  Pallas kernels: 0 us -> 92.6 us
  blocking collectives: 72 us -> 0 us
  local copies, waits for them, and re-layouts: 31.1 us -> 5.48 us
  other arithmetic: 21.6 us -> 0.6 us
  matrix products: 20.9 us -> 0 us
  between operations: 15.9 us -> 0.92 us
    reduce_scatter x2 -> x0, waiting for transfers between devices: 242 us -> none  [the longest x1 210 us: trans_part(): lax.psum_scatter(cross, 'samp', scatter_dimension=1, tiled=True)]
    pallas_call x0 -> x7, Pallas kernels: none -> 92.6 us  [the longest x1 49.1 us: gather_proteins(): pl.pallas_call(protein_kernel, out_shape=[jax.ShapeDtypeStruct((4, 2, PB,...]
    all_gather x1 -> x0, blocking collectives: 38.8 us -> none  [cis_part(): full_block = lax.all_gather(proteins, 'samp', axis=0, tiled=True)]
    psum x2 -> x0, blocking collectives: 33.2 us -> none  [the longest x1 27.9 us: cis_part(): return lax.psum(column_sums, ('var', 'samp'))]
    gather x3 -> x0, local copies, waits for them, and re-layouts: 23.4 us -> none  [the longest x2 20.8 us: cis_part(): permuted = jnp.take(full_block, perm_table, axis=0)]
    dot_general x2 -> x0, matrix products: 20.9 us -> none  [the longest x1 16.1 us: trans_part(): product = jnp.dot(genotype, slab_piece, preferred_element_type=jnp.float32)]
    reduce_sum x5 -> x0, other arithmetic: 10.4 us -> none  [the longest x1 4.46 us: trans_part(): jnp.sum(widened, 0)]
    all_to_all x1 -> x0, starting transfers between devices: 8.58 us -> none  [cis_part(): lax.all_to_all(chosen, 'prot', split_axis=0, concat_axis=0, tiled=True)]
  transfers between devices with their start and end apart: 6 -> 5, of which waited for: 4 -> 0; matrix products, arithmetic and copies ran while one was open for 16% -> 1% of each run, Pallas kernels for 0% -> 83%
where the time goes in v2:
time: 105 us
  Pallas kernels  92.6 us (88%)
  local copies, waits for them, and re-layouts  5.48 us (5%)
  starting transfers between devices  5.09 us (5%)
    pallas_call x1, Pallas kernels, gather_proteins(): pl.pallas_call(protein_kernel, out_shape=[jax.ShapeDtypeStruct((4, 2, PB,...  49.1 us
    pallas_call x1, Pallas kernels, cis(): pl.pallas_call(cis_kernel, out_shape=[jax.ShapeDtypeStruct((4, 256), jnp....  22.4 us
    pallas_call x3, Pallas kernels, trans(): pl.pallas_call(functools.partial(trans_kernel, chunks, first, last, len(a...  18.9 us
    unnamed x14, local copies, waits for them, and re-layouts  5.48 us
    ppermute x4, starting transfers between devices, body(): got = [lax.ppermute(chunk, 'samp', SWAP) for chunk in mine]  4.99 us
  transfers between devices with their start and end apart: 5, of which 0 were waited for; matrix products, arithmetic and copies ran while one was open for 1% of the time, Pallas kernels for 83%

profile of v2, /device:TPU:1, one launch (start us, length us, event | category | flops | bytes accessed | tf_op | source)
XLA Modules:
  0.0 104.7 jit_solution(2167164196887052590)
XLA Ops:
  0.6 0.0 copy-start
  0.6 1.9 %copy-done = bf16[1536,1024]{1,0:T(8,128)(2,1)S(1)} copy-done((bf16[1536,1024]{1,0:T(8,128)(2,1)S(1)}, bf16[1536,1024]{1,0:T(8,128)(2,1)}, u32[]{:S(2)}) %copy-start) | copy-done | bytes 3145752
  2.5 0.0 copy-start.2
  2.5 0.7 copy-done.2
  3.2 1.7 %sort_blocks.1 = (bf16[512,1024]{1,0:T(8,128)(2,1)S(1)}, bf16[512,1024]{1,0:T(8,128)(2,1)S(1)}, bf16[256,1024]{1,0:T(8,128)(2,1)S(1)}, bf16[256,1024]{1,0:T(8,12...) custom-call(s32[1,16]{1,0:T(1,128)S(1)} %copy-done.2, bf16[1536,1024]{1,0:T(8,128)(2,1)S(1)} %copy-done), custom_call_target="tpu_custom_call" | custom-call | tf_op jit(solution)/shard_map/sort_blocks/pallas_call | solution.py:81
  4.8 0.0 copy-start.3
  4.9 2.1 %collective-permute-start.1 = (bf16[512,1024]{1,0:T(8,128)(2,1)S(1)}, bf16[512,1024]{1,0:T(8,128)(2,1)S(1)}, u32[]{:S(2)}, u32[]{:S(2)}) collective-permute-start(bf16[512,1024]{1,0:T(8,128)(2,1)S(1)} %get-tuple-element.15), channel_id=1, source_target_pairs={{0,1},{1,0},{2,3},{3,2},{4,5},{5,4},{6,7},{7,6},{8,9},{9,8},{10,11... | collective-permute-start | bytes 3145736 | tf_op jit(solution)/shard_map/ppermute | solution.py:534
  7.0 0.1 collective-permute-start
  7.1 1.4 %collective-permute-start.3 = (bf16[256,1024]{1,0:T(8,128)(2,1)S(1)}, bf16[256,1024]{1,0:T(8,128)(2,1)S(1)}, u32[]{:S(2)}, u32[]{:S(2)}) collective-permute-start(bf16[256,1024]{1,0:T(8,128)(2,1)S(1)} %get-tuple-element.19), channel_id=1, source_target_pairs={{0,1},{1,0},{2,3},{3,2},{4,5},{5,4},{6,7},{7,6},{8,9},{9,8},{10,11... | collective-permute-start | bytes 1572872 | tf_op jit(solution)/shard_map/ppermute | solution.py:534
  8.5 0.1 collective-permute-start.4
  8.6 1.4 %collective-permute-start.2 = (bf16[512,1024]{1,0:T(8,128)(2,1)S(1)}, bf16[512,1024]{1,0:T(8,128)(2,1)S(1)}, u32[]{:S(2)}, u32[]{:S(2)}) collective-permute-start(bf16[512,1024]{1,0:T(8,128)(2,1)S(1)} %get-tuple-element.18), channel_id=1, source_target_pairs={{0,1},{1,0},{2,3},{3,2},{4,5},{5,4},{6,7},{7,6},{8,9},{9,8},{10,11... | collective-permute-start | bytes 3145736 | tf_op jit(solution)/shard_map/ppermute | solution.py:534
  9.9 0.0 copy-start.5
  10.0 1.0 copy-done.5
  10.9 0.0 copy-start.6
  10.9 0.7 copy-done.6
  11.7 49.1 %gather_proteins.1 = (bf16[4,2,184,2048]{3,2,1,0:T(8,128)(2,1)S(1)}, bf16[8,256,2048]{2,1,0:T(8,128)(2,1)S(1)}) custom-call(bf16[184,1024]{1,0:T(8,128)(2,1)S(1)} %bitcast.12, s32[4,1024]{1,0:T(4,128)S(1)} %copy-done.6, bf16[512,1024]{1,0:T(8,128)(2,1)S(1)} %get-tuple-element.13.chosen.chosen_own), custom_call_target="tpu_custom_call" | custom-call | flops 8999999488 | bytes 83886080 | tf_op jit(solution)/shard_map/gather_proteins/pallas_call | solution.py:303
  60.7 0.0 copy-done.3
  60.7 0.0 collective-permute-done.1.got.refs_0_
  60.7 0.6 choose.1.chosen
  61.4 0.0 collective-permute-done.perm
  61.4 0.0 copy-start.4
  61.4 1.2 %copy-done.4 = bf16[512,1024]{1,0:T(8,128)(2,1)S(1)} copy-done((bf16[512,1024]{1,0:T(8,128)(2,1)S(1)}, bf16[512,1024]{1,0:T(8,128)(2,1)}, u32[]{:S(2)}) %copy-start.4) | copy-done | bytes 1048600
  62.6 0.0 copy-start.1
  62.6 22.4 %cis.1 = (f32[4,256]{1,0:T(4,128)S(1)}, f32[2,8,184,128]{3,2,1,0:T(8,128)S(1)}) custom-call(s32[64]{0:T(128)S(1)} %get-tuple-element.12.plan, s32[4,1024]{1,0:T(4,128)S(1)} %collective-permute-done.perm, bf16[8,184,2048]{2,1,0:T(8,128)(2,1)S(1)} %bitcast.5, bf16[512,1024]{1,0:T(8,128)(2,1)S(1)} %copy-done.4, bf16[512,1024]{1,0:T(8,128)(2,1)S(1)} %choose.1.chosen, ...), custom_call_target="tpu_custom_call" | custom-call | flops 12000000000 | bytes 20971520 | tf_op jit(solution)/shard_map/cis/pallas_call | solution.py:430
  85.0 0.0 collective-permute-done.2.refs_1_
  85.0 0.0 copy-done.1
  85.1 11.4 %trans.3.refs_3_ = bf16[1472,1536]{1,0:T(8,128)(2,1)} custom-call(s32[64]{0:T(128)S(1)} %get-tuple-element.12.plan, bf16[1472,2048]{1,0:T(8,128)(2,1)S(1)} %bitcast.6, f32[2,1472,128]{2,1,0:T(8,128)S(1)} %bitcast.9, bf16[1536,1024]{1,0:T(8,128)(2,1)S(1)} %copy-done.1, bf16[512,1024]{1,0:T(8,128)(2,1)S(1)} %collective-permute-done.1.got.refs_0_, ...), custom_call_target="tpu_custom_call" | custom-call | flops 6174015488 | bytes 8388608 | tf_op jit(solution)/shard_map/trans/pallas_call | solution.py:509
  96.5 0.0 collective-permute-done.3.refs_2_
  96.5 3.8 %trans.4.refs_4_ = bf16[1472,1536]{1,0:T(8,128)(2,1)} custom-call(s32[64]{0:T(128)S(1)} %get-tuple-element.12.plan, bf16[1472,2048]{1,0:T(8,128)(2,1)S(1)} %bitcast.7, f32[2,1472,128]{2,1,0:T(8,128)S(1)} %bitcast.10, bf16[1536,1024]{1,0:T(8,128)(2,1)S(1)} %copy-done.1, ...), custom_call_target="tpu_custom_call", output_to_operand_aliasing={{}: (7, {})} | custom-call | flops 1543503872 | bytes 8388608 | tf_op jit(solution)/shard_map/trans/pallas_call | solution.py:509
  100.3 0.6 slice_multiply_fusion
  100.9 0.0 collective-permute-done.4.refs_3_
  100.9 3.7 %trans.5 = bf16[1472,1536]{1,0:T(8,128)(2,1)} custom-call(s32[64]{0:T(128)S(1)} %get-tuple-element.12.plan, bf16[1472,2048]{1,0:T(8,128)(2,1)S(1)} %bitcast.8, f32[2,1472,128]{2,1,0:T(8,128)S(1)} %bitcast.11, bf16[1536,1024]{1,0:T(8,128)(2,1)S(1)} %copy-done.1, ...), custom_call_target="tpu_custom_call", output_to_operand_aliasing={{}: (8, {})} | custom-call | flops 1543503872 | bytes 8388608 | tf_op jit(solution)/shard_map/trans/pallas_call | solution.py:509
Async XLA Ops:
  0.6 1.9 %copy-start = (bf16[1536,1024]{1,0:T(8,128)(2,1)S(1)}, bf16[1536,1024]{1,0:T(8,128)(2,1)}, u32[]{:S(2)}) copy-start(bf16[1536,1024]{1,0:T(8,128)(2,1)} %g_ref.7) | copy-start | bytes 9437188
  2.5 0.7 copy-start.2
  4.8 55.9 %copy-start.3 = (bf16[512,1024]{1,0:T(8,128)(2,1)}, bf16[512,1024]{1,0:T(8,128)(2,1)S(1)}, u32[]{:S(2)}) copy-start(bf16[512,1024]{1,0:T(8,128)(2,1)S(1)} %get-tuple-element.13.chosen.chosen_own) | copy-start | bytes 3145732
  4.9 55.9 %collective-permute-start.1 = (bf16[512,1024]{1,0:T(8,128)(2,1)S(1)}, bf16[512,1024]{1,0:T(8,128)(2,1)S(1)}, u32[]{:S(2)}, u32[]{:S(2)}) collective-permute-start(bf16[512,1024]{1,0:T(8,128)(2,1)S(1)} %get-tuple-element.15), channel_id=1, source_target_pairs={{0,1},{1,0},{2,3},{3,2},{4,5},{5,4},{6,7},{7,6},{8,9},{9,8},{10,11... | collective-permute-start | bytes 3145736 | tf_op jit(solution)/shard_map/ppermute | solution.py:534
  7.0 54.4 %collective-permute-start = (s32[4,1024]{1,0:T(4,128)}, s32[4,1024]{1,0:T(4,128)S(1)}, u32[]{:S(2)}, u32[]{:S(2)}) collective-permute-start(s32[4,1024]{1,0:T(4,128)} %perm.1), channel_id=1, source_target_pairs={{0,1},{1,0},{2,3},{3,2},{4,5},{5,4},{6,7},{7,6},{8,9},{9,8},{10,11... | collective-permute-start | bytes 49160 | tf_op jit(solution)/shard_map/ppermute | solution.py:532
  7.1 89.4 %collective-permute-start.3 = (bf16[256,1024]{1,0:T(8,128)(2,1)S(1)}, bf16[256,1024]{1,0:T(8,128)(2,1)S(1)}, u32[]{:S(2)}, u32[]{:S(2)}) collective-permute-start(bf16[256,1024]{1,0:T(8,128)(2,1)S(1)} %get-tuple-element.19), channel_id=1, source_target_pairs={{0,1},{1,0},{2,3},{3,2},{4,5},{5,4},{6,7},{7,6},{8,9},{9,8},{10,11... | collective-permute-start | bytes 1572872 | tf_op jit(solution)/shard_map/ppermute | solution.py:534
  8.5 92.5 %collective-permute-start.4 = (bf16[256,1024]{1,0:T(8,128)(2,1)S(1)}, bf16[256,1024]{1,0:T(8,128)(2,1)S(1)}, u32[]{:S(2)}, u32[]{:S(2)}) collective-permute-start(bf16[256,1024]{1,0:T(8,128)(2,1)S(1)} %get-tuple-element.20), channel_id=1, source_target_pairs={{0,1},{1,0},{2,3},{3,2},{4,5},{5,4},{6,7},{7,6},{8,9},{9,8},{10,11... | collective-permute-start | bytes 1572872 | tf_op jit(solution)/shard_map/ppermute | solution.py:534
  8.6 76.5 %collective-permute-start.2 = (bf16[512,1024]{1,0:T(8,128)(2,1)S(1)}, bf16[512,1024]{1,0:T(8,128)(2,1)S(1)}, u32[]{:S(2)}, u32[]{:S(2)}) collective-permute-start(bf16[512,1024]{1,0:T(8,128)(2,1)S(1)} %get-tuple-element.18), channel_id=1, source_target_pairs={{0,1},{1,0},{2,3},{3,2},{4,5},{5,4},{6,7},{7,6},{8,9},{9,8},{10,11... | collective-permute-start | bytes 3145736 | tf_op jit(solution)/shard_map/ppermute | solution.py:534
  9.9 1.0 copy-start.5
  10.9 0.7 copy-start.6
  61.4 1.2 %copy-start.4 = (bf16[512,1024]{1,0:T(8,128)(2,1)S(1)}, bf16[512,1024]{1,0:T(8,128)(2,1)}, u32[]{:S(2)}) copy-start(bf16[512,1024]{1,0:T(8,128)(2,1)} %copy-done.3) | copy-start | bytes 3145732
  62.6 22.4 %copy-start.1 = (bf16[1536,1024]{1,0:T(8,128)(2,1)S(1)}, bf16[1536,1024]{1,0:T(8,128)(2,1)}, u32[]{:S(2)}) copy-start(bf16[1536,1024]{1,0:T(8,128)(2,1)} %g_ref.7) | copy-start | bytes 9437188

commit v3 on v2

--- a/solution.py
+++ b/solution.py
@@ -16,9 +16,9 @@
 ALL = 2 * HALF
 PB = 184
 COLS = 8 * PB
-CHUNKS = (8, 8, 4, 4)
+CHUNKS = (8, 16)
 STARTS = tuple(sum(CHUNKS[:c]) for c in range(len(CHUNKS)))
-GROUPS = ((2, 0, 8), (3, 8, 10), (4, 10, 12))
+GROUPS = ((2, 0, 12),)
 EPS = 1e-6
 N = float(ALL)
 MIB = 1 << 20
@@ -177,15 +177,15 @@
     def far_all(y2):
         return data.at[y2, c, :, pl.ds(HALF, HALF)]
 
-    def pass_near(t, k, downward=True):
+    def pass_near(t, k):
         y2 = (y + 4 - k) % 4
-        here = near(y2, (z + 8 - t) % 8)
-        send(here, here, sa.at[0, t, k], ra.at[0, t, k], up)
-
-        @pl.when(t < 3)
-        def _():
-            here = near(y2, (z + t) % 8)
-            send(here, here, sa.at[1, t, k], ra.at[1, t, k], down)
+
+        def go(way):
+            here = near(y2, (z + (8 - t, t)[way]) % 8)
+            send(here, here, sa.at[way, t, k], ra.at[way, t, k], (up, down)[way])
+
+        go(k // 2)
+        pl.when(t < 3)(lambda: go(1 - k // 2))
 
     def pass_far(t):
         here = far(y, (z + 8 - t) % 8)
@@ -216,11 +216,12 @@
         spread_far(7 - t)
         for k in range(4):
             y2 = (y + 4 - k) % 4
-            arrived(near(y2, (z + 7 - t) % 8), ra.at[0, t, k])
+            way = k // 2
+            arrived(near(y2, (z + (7 - t, 1 + t)[way]) % 8), ra.at[way, t, k])
 
             @pl.when(t < 3)
             def _():
-                arrived(near(y2, (z + 1 + t) % 8), ra.at[1, t, k])
+                arrived(near(y2, (z + (1 + t, 7 - t)[way]) % 8), ra.at[1 - way, t, k])
                 pass_near(t + 1, k)
 
         share(near_all((z + 7 - t) % 8), 1 + t)
@@ -289,8 +290,10 @@
     for t in range(4):
         for way in range(2 if t < 3 else 1):
             left(one, sb.at[way, t])
-            for k in range(4):
-                left(one, sa.at[way, t, k])
+        for k in range(4):
+            left(one, sa.at[k // 2, t, k])
+            if t < 3:
+                left(one, sa.at[1 - k // 2, t, k])
     for k in range(8):
         left(near_all(z), sd.at[k])
     for k in range(8, 12):
@@ -313,7 +316,7 @@
             dma, dma((2,)), dma((2,)), dma((3,)), dma((3,)), dma((2, 4, 4)), dma((2, 4, 4)),
             dma((2, 4)), dma((2, 4)), dma((3, 8)), dma((3, 8)), dma((12,)), dma((12,)),
         ],
-        compiler_params=pltpu.CompilerParams(collective_id=1, has_side_effects=True, vmem_limit_bytes=24 * MIB),
+        compiler_params=pltpu.CompilerParams(collective_id=1, has_side_effects=True, vmem_limit_bytes=18 * MIB),
         cost_estimate=pl.CostEstimate(flops=9_000_000_000, bytes_accessed=80 * MIB, transcendentals=0),
         name="gather_proteins",
     )(prot, perm, chosen)
@@ -444,7 +447,7 @@
             pltpu.VMEM((16, 4, 256), jnp.float32),
             dma((2, 8)), dma((2, 8)), dma((2, 2, 8)), dma((16,)),
         ],
-        compiler_params=pltpu.CompilerParams(collective_id=2, has_side_effects=True, vmem_limit_bytes=36 * MIB),
+        compiler_params=pltpu.CompilerParams(collective_id=2, has_side_effects=True, vmem_limit_bytes=30 * MIB),
         cost_estimate=pl.CostEstimate(flops=12_000_000_000, bytes_accessed=20 * MIB, transcendentals=0),
         name="cis",
     )(plan, perm, prot, chosen_own, chosen_got, moved)
@@ -517,7 +520,7 @@
             pltpu.SemaphoreType.DMA((2, 2)),
         ],
         input_output_aliases=aliases,
-        compiler_params=pltpu.CompilerParams(vmem_limit_bytes=24 * MIB),
+        compiler_params=pltpu.CompilerParams(vmem_limit_bytes=20 * MIB),
         cost_estimate=pl.CostEstimate(
             flops=2 * COLS * ALL * 128 * (last - first), bytes_accessed=8 * MIB, transcendentals=0
         ),

time: 105 us -> 97.2 us (0.926)
  Pallas kernels: 92.6 us -> 89.6 us
  local copies, waits for them, and re-layouts: 5.48 us -> 2.55 us
  starting transfers between devices: 5.09 us -> 3.59 us
    unnamed x14 -> x10, local copies, waits for them, and re-layouts: 5.48 us -> 2.55 us
    pallas_call x3 -> x1, Pallas kernels: 18.9 us -> 16.4 us  [trans(): pl.pallas_call(functools.partial(trans_kernel, chunks, first, last, len(a...]
    pallas_call x1, Pallas kernels: 49.1 us -> 47.1 us  [gather_proteins(): pl.pallas_call(protein_kernel, out_shape=[jax.ShapeDtypeStruct((4, 2, PB,...]
    ppermute x4 -> x2, starting transfers between devices: 4.99 us -> 3.49 us  [body(): got = [lax.ppermute(chunk, 'samp', SWAP) for chunk in mine]]
    pallas_call x1, Pallas kernels: 22.4 us -> 23.8 us  [cis(): pl.pallas_call(cis_kernel, out_shape=[jax.ShapeDtypeStruct((4, 256), jnp....]
  transfers between devices with their start and end apart: 5 -> 3, of which waited for: 0 -> 0; matrix products, arithmetic and copies ran while one was open for 1% -> 1% of each run, Pallas kernels for 83% -> 74%
where the time goes in v3:
time: 97.2 us; the launch traced here: 97 us
  Pallas kernels  89.6 us (92%)
  starting transfers between devices  3.59 us (4%)
  local copies, waits for them, and re-layouts  2.55 us (3%)
    pallas_call x1, Pallas kernels, gather_proteins(): pl.pallas_call(protein_kernel, out_shape=[jax.ShapeDtypeStruct((4, 2, PB,...  47.1 us
    pallas_call x1, Pallas kernels, cis(): pl.pallas_call(cis_kernel, out_shape=[jax.ShapeDtypeStruct((4, 256), jnp....  23.8 us
    pallas_call x1, Pallas kernels, trans(): pl.pallas_call(functools.partial(trans_kernel, chunks, first, last, len(a...  16.4 us
    ppermute x2, starting transfers between devices, body(): got = [lax.ppermute(chunk, 'samp', SWAP) for chunk in mine]  3.49 us
    unnamed x10, local copies, waits for them, and re-layouts  2.55 us
  transfers between devices with their start and end apart: 3, of which 0 were waited for; matrix products, arithmetic and copies ran while one was open for 1% of the time, Pallas kernels for 74%

profile of v3, /device:TPU:1, one launch (start us, length us, event | category | flops | bytes accessed | tf_op | source)
XLA Modules:
  0.0 97.0 jit_solution(17231294080916994244)
XLA Ops:
  0.6 0.0 copy-start
  0.6 1.9 %copy-done = bf16[1536,1024]{1,0:T(8,128)(2,1)S(1)} copy-done((bf16[1536,1024]{1,0:T(8,128)(2,1)S(1)}, bf16[1536,1024]{1,0:T(8,128)(2,1)}, u32[]{:S(2)}) %copy-start) | copy-done | bytes 3145752
  2.5 0.0 copy-start.2
  2.5 0.7 copy-done.2
  3.2 0.0 copy-start.4
  3.2 0.0 copy-start.3
  3.2 1.7 %sort_blocks.1 = (bf16[512,1024]{1,0:T(8,128)(2,1)S(1)}, bf16[1024,1024]{1,0:T(8,128)(2,1)S(1)}, bf16[512,1024]{1,0:T(8,128)(2,1)S(1)}, s32[64]{0:T(128)S(1)}) custom-call(s32[1,16]{1,0:T(1,128)S(1)} %copy-done.2, bf16[1536,1024]{1,0:T(8,128)(2,1)S(1)} %copy-done), custom_call_target="tpu_custom_call" | custom-call | tf_op jit(solution)/shard_map/sort_blocks/pallas_call | solution.py:81
  4.8 2.1 %collective-permute-start.1 = (bf16[512,1024]{1,0:T(8,128)(2,1)S(1)}, bf16[512,1024]{1,0:T(8,128)(2,1)S(1)}, u32[]{:S(2)}, u32[]{:S(2)}) collective-permute-start(bf16[512,1024]{1,0:T(8,128)(2,1)S(1)} %get-tuple-element.13), channel_id=1, source_target_pairs={{0,1},{1,0},{2,3},{3,2},{4,5},{5,4},{6,7},{7,6},{8,9},{9,8},{10,11... | collective-permute-start | bytes 3145736 | tf_op jit(solution)/shard_map/ppermute | solution.py:537
  7.0 0.0 copy-done.4
  7.0 0.1 collective-permute-start
  7.1 1.4 %collective-permute-start.2 = (bf16[1024,1024]{1,0:T(8,128)(2,1)S(1)}, bf16[1024,1024]{1,0:T(8,128)(2,1)S(1)}, u32[]{:S(2)}, u32[]{:S(2)}) collective-permute-start(bf16[1024,1024]{1,0:T(8,128)(2,1)S(1)} %get-tuple-element.16), channel_id=1, source_target_pairs={{0,1},{1,0},{2,3},{3,2},{4,5},{5,4},{6,7},{7,6},{8,9},{9,8},{10,11... | collective-permute-start | bytes 6291464 | tf_op jit(solution)/shard_map/ppermute | solution.py:537
  8.4 0.0 copy-done.3
  8.4 47.1 %gather_proteins.1 = (bf16[4,2,184,2048]{3,2,1,0:T(8,128)(2,1)S(1)}, bf16[8,256,2048]{2,1,0:T(8,128)(2,1)S(1)}) custom-call(bf16[184,1024]{1,0:T(8,128)(2,1)S(1)} %bitcast.5, s32[4,1024]{1,0:T(4,128)S(1)} %copy-done.4, bf16[512,1024]{1,0:T(8,128)(2,1)S(1)} %get-tuple-element.11.chosen.chosen_own), custom_call_target="tpu_custom_call" | custom-call | flops 8999999488 | bytes 83886080 | tf_op jit(solution)/shard_map/gather_proteins/pallas_call | solution.py:306
  55.6 0.0 collective-permute-done.1.got.refs_0_
  55.6 0.6 choose.1.chosen
  56.2 0.0 collective-permute-done.perm
  56.2 0.0 copy-start.1
  56.2 23.8 %cis.1 = (f32[4,256]{1,0:T(4,128)S(1)}, f32[2,8,184,128]{3,2,1,0:T(8,128)S(1)}) custom-call(s32[64]{0:T(128)S(1)} %get-tuple-element.10.plan, s32[4,1024]{1,0:T(4,128)S(1)} %collective-permute-done.perm, bf16[8,184,2048]{2,1,0:T(8,128)(2,1)S(1)} %bitcast.6, bf16[512,1024]{1,0:T(8,128)(2,1)S(1)} %get-tuple-element.11.chosen.chosen_own, ...), custom_call_target="tpu_custom_call" | custom-call | flops 12000000000 | bytes 20971520 | tf_op jit(solution)/shard_map/cis/pallas_call | solution.py:433
  80.0 0.6 slice_multiply_fusion
  80.6 0.0 collective-permute-done.2.refs_1_
  80.6 0.0 copy-done.1
  80.6 16.4 %trans.1 = bf16[1472,1536]{1,0:T(8,128)(2,1)} custom-call(s32[64]{0:T(128)S(1)} %get-tuple-element.10.plan, bf16[1472,2048]{1,0:T(8,128)(2,1)S(1)} %bitcast.7, f32[2,1472,128]{2,1,0:T(8,128)S(1)} %bitcast.8, bf16[1536,1024]{1,0:T(8,128)(2,1)S(1)} %copy-done.1, bf16[512,1024]{1,0:T(8,128)(2,1)S(1)} %collective-permute-done.1.got.refs_0_, ...), custom_call_target="tpu_custom_call" | custom-call | flops 9261023232 | bytes 8388608 | tf_op jit(solution)/shard_map/trans/pallas_call | solution.py:512
Async XLA Ops:
  0.6 1.9 %copy-start = (bf16[1536,1024]{1,0:T(8,128)(2,1)S(1)}, bf16[1536,1024]{1,0:T(8,128)(2,1)}, u32[]{:S(2)}) copy-start(bf16[1536,1024]{1,0:T(8,128)(2,1)} %g_ref.3) | copy-start | bytes 9437188
  2.5 0.7 copy-start.2
  3.2 3.8 %copy-start.4 = (s32[4,1024]{1,0:T(4,128)S(1)}, s32[4,1024]{1,0:T(4,128)}, u32[]{:S(2)}) copy-start(s32[4,1024]{1,0:T(4,128)} %perm.1) | copy-start | bytes 49156
  3.2 5.3 %copy-start.3 = (bf16[1024,184]{0,1:T(8,128)(2,1)S(1)}, bf16[1024,184]{0,1:T(8,128)(2,1)}, u32[]{:S(2)}) copy-start(bf16[1024,184]{0,1:T(8,128)(2,1)} %param.5) | copy-start | bytes 1130500
  4.8 50.7 %collective-permute-start.1 = (bf16[512,1024]{1,0:T(8,128)(2,1)S(1)}, bf16[512,1024]{1,0:T(8,128)(2,1)S(1)}, u32[]{:S(2)}, u32[]{:S(2)}) collective-permute-start(bf16[512,1024]{1,0:T(8,128)(2,1)S(1)} %get-tuple-element.13), channel_id=1, source_target_pairs={{0,1},{1,0},{2,3},{3,2},{4,5},{5,4},{6,7},{7,6},{8,9},{9,8},{10,11... | collective-permute-start | bytes 3145736 | tf_op jit(solution)/shard_map/ppermute | solution.py:537
  7.0 49.2 %collective-permute-start = (s32[4,1024]{1,0:T(4,128)S(1)}, s32[4,1024]{1,0:T(4,128)S(1)}, u32[]{:S(2)}, u32[]{:S(2)}) collective-permute-start(s32[4,1024]{1,0:T(4,128)S(1)} %copy-done.4), channel_id=1, source_target_pairs={{0,1},{1,0},{2,3},{3,2},{4,5},{5,4},{6,7},{7,6},{8,9},{9,8},{10,11... | collective-permute-start | bytes 49160 | tf_op jit(solution)/shard_map/ppermute | solution.py:535
  7.1 73.5 %collective-permute-start.2 = (bf16[1024,1024]{1,0:T(8,128)(2,1)S(1)}, bf16[1024,1024]{1,0:T(8,128)(2,1)S(1)}, u32[]{:S(2)}, u32[]{:S(2)}) collective-permute-start(bf16[1024,1024]{1,0:T(8,128)(2,1)S(1)} %get-tuple-element.16), channel_id=1, source_target_pairs={{0,1},{1,0},{2,3},{3,2},{4,5},{5,4},{6,7},{7,6},{8,9},{9,8},{10,11... | collective-permute-start | bytes 6291464 | tf_op jit(solution)/shard_map/ppermute | solution.py:537
  56.2 24.4 %copy-start.1 = (bf16[1536,1024]{1,0:T(8,128)(2,1)S(1)}, bf16[1536,1024]{1,0:T(8,128)(2,1)}, u32[]{:S(2)}) copy-start(bf16[1536,1024]{1,0:T(8,128)(2,1)} %g_ref.3) | copy-start | bytes 9437188

commit v4 on v3

--- a/solution.py
+++ b/solution.py
@@ -455,7 +455,9 @@
 
 def trans_kernel(chunks, first, last, aliased, plan, prot, stat, g_ref, *refs):
     got = refs[:chunks]
-    out, rows, stage, sems = refs[chunks + aliased :]
+    out, rows, halves, stage, sems = refs[chunks + aliased :]
+    for c in range(chunks):
+        halves[STARTS[c] * VB : (STARTS[c] + CHUNKS[c]) * VB, :] = got[c][...]
     steps = (last - first) // 2
 
     def copy_out(n, h):
@@ -465,30 +467,24 @@
         )
 
     def step(n, _):
+        @pl.when(n >= 2)
+        def _():
+            for h in range(2):
+                copy_out(n - 2, h).wait()
+
         for t in range(2):
             tile = plan[PLAN_TILE + first + 2 * n + t]
             at = t * 128
             rows[at : at + 128, :HALF] = g_ref[pl.ds(pl.multiple_of(tile * 128, 128), 128), :]
             for h in range(2):
-                place = plan[tile * 2 + h]
-                for c in range(chunks):
-
-                    @pl.when((place >= STARTS[c]) & (place < STARTS[c] + CHUNKS[c]))
-                    def _():
-                        row = pl.multiple_of((place - STARTS[c]) * VB, VB)
-                        rows[at + h * VB : at + (h + 1) * VB, HALF:] = got[c][pl.ds(row, VB), :]
+                row = pl.multiple_of(plan[tile * 2 + h] * VB, VB)
+                rows[at + h * VB : at + (h + 1) * VB, HALF:] = halves[pl.ds(row, VB), :]
 
         both = rows[...]
         by, off = as_rows(*scales(both[:, :HALF], both[:, HALF:]))
         cross = dot_nt(prot[...], both)
         mean = jnp.concatenate([stat[0], stat[0]], 1)
         inv = jnp.concatenate([stat[1], stat[1]], 1)
-
-        @pl.when(n >= 2)
-        def _():
-            for h in range(2):
-                copy_out(n - 2, h).wait()
-
         stage[n % 2] = ((cross * by - mean * off) * inv).astype(jnp.bfloat16)
         for h in range(2):
             copy_out(n, h).start()
@@ -516,6 +512,7 @@
         out_specs=hbm,
         scratch_shapes=[
             pltpu.VMEM((256, ALL), jnp.bfloat16),
+            pltpu.VMEM((ROWS, HALF), jnp.bfloat16),
             pltpu.VMEM((2, COLS, 256), jnp.bfloat16),
             pltpu.SemaphoreType.DMA((2, 2)),
         ],

time: 97.2 us -> 95 us (0.977)
  Pallas kernels: 89.6 us -> 87.5 us
    pallas_call x1, Pallas kernels: 16.4 us -> 14.3 us  [trans(): pl.pallas_call(functools.partial(trans_kernel, chunks, first, last, len(a...]
  transfers between devices with their start and end apart: 3 -> 3, of which waited for: 0 -> 0; matrix products, arithmetic and copies ran while one was open for 1% -> 1% of each run, Pallas kernels for 74% -> 75%
where the time goes in v4:
time: 95 us; the launch traced here: 94.9 us
  Pallas kernels  87.5 us (92%)
  starting transfers between devices  3.59 us (4%)
  local copies, waits for them, and re-layouts  2.55 us (3%)
    pallas_call x1, Pallas kernels, gather_proteins(): pl.pallas_call(protein_kernel, out_shape=[jax.ShapeDtypeStruct((4, 2, PB,...  47.1 us
    pallas_call x1, Pallas kernels, cis(): pl.pallas_call(cis_kernel, out_shape=[jax.ShapeDtypeStruct((4, 256), jnp....  23.8 us
    pallas_call x1, Pallas kernels, trans(): pl.pallas_call(functools.partial(trans_kernel, chunks, first, last, len(a...  14.3 us
    ppermute x2, starting transfers between devices, body(): got = [lax.ppermute(chunk, 'samp', SWAP) for chunk in mine]  3.49 us
    unnamed x10, local copies, waits for them, and re-layouts  2.55 us
  transfers between devices with their start and end apart: 3, of which 0 were waited for; matrix products, arithmetic and copies ran while one was open for 1% of the time, Pallas kernels for 75%

profile of v4, /device:TPU:1, one launch (start us, length us, event | category | flops | bytes accessed | tf_op | source)
XLA Modules:
  0.0 94.9 jit_solution(10182601549899112061)
XLA Ops:
  0.6 0.0 copy-start
  0.6 1.9 %copy-done = bf16[1536,1024]{1,0:T(8,128)(2,1)S(1)} copy-done((bf16[1536,1024]{1,0:T(8,128)(2,1)S(1)}, bf16[1536,1024]{1,0:T(8,128)(2,1)}, u32[]{:S(2)}) %copy-start) | copy-done | bytes 3145752
  2.5 0.0 copy-start.2
  2.5 0.7 copy-done.2
  3.2 0.0 copy-start.4
  3.2 0.0 copy-start.3
  3.2 1.7 %sort_blocks.1 = (bf16[512,1024]{1,0:T(8,128)(2,1)S(1)}, bf16[1024,1024]{1,0:T(8,128)(2,1)S(1)}, bf16[512,1024]{1,0:T(8,128)(2,1)S(1)}, s32[64]{0:T(128)S(1)}) custom-call(s32[1,16]{1,0:T(1,128)S(1)} %copy-done.2, bf16[1536,1024]{1,0:T(8,128)(2,1)S(1)} %copy-done), custom_call_target="tpu_custom_call" | custom-call | tf_op jit(solution)/shard_map/sort_blocks/pallas_call | solution.py:81
  4.8 2.1 %collective-permute-start.1 = (bf16[512,1024]{1,0:T(8,128)(2,1)S(1)}, bf16[512,1024]{1,0:T(8,128)(2,1)S(1)}, u32[]{:S(2)}, u32[]{:S(2)}) collective-permute-start(bf16[512,1024]{1,0:T(8,128)(2,1)S(1)} %get-tuple-element.13), channel_id=1, source_target_pairs={{0,1},{1,0},{2,3},{3,2},{4,5},{5,4},{6,7},{7,6},{8,9},{9,8},{10,11... | collective-permute-start | bytes 3145736 | tf_op jit(solution)/shard_map/ppermute | solution.py:534
  7.0 0.0 copy-done.4
  7.0 0.1 collective-permute-start
  7.1 1.4 %collective-permute-start.2 = (bf16[1024,1024]{1,0:T(8,128)(2,1)S(1)}, bf16[1024,1024]{1,0:T(8,128)(2,1)S(1)}, u32[]{:S(2)}, u32[]{:S(2)}) collective-permute-start(bf16[1024,1024]{1,0:T(8,128)(2,1)S(1)} %get-tuple-element.16), channel_id=1, source_target_pairs={{0,1},{1,0},{2,3},{3,2},{4,5},{5,4},{6,7},{7,6},{8,9},{9,8},{10,11... | collective-permute-start | bytes 6291464 | tf_op jit(solution)/shard_map/ppermute | solution.py:534
  8.4 0.0 copy-done.3
  8.4 47.1 %gather_proteins.1 = (bf16[4,2,184,2048]{3,2,1,0:T(8,128)(2,1)S(1)}, bf16[8,256,2048]{2,1,0:T(8,128)(2,1)S(1)}) custom-call(bf16[184,1024]{1,0:T(8,128)(2,1)S(1)} %bitcast.5, s32[4,1024]{1,0:T(4,128)S(1)} %copy-done.4, bf16[512,1024]{1,0:T(8,128)(2,1)S(1)} %get-tuple-element.11.chosen.chosen_own), custom_call_target="tpu_custom_call" | custom-call | flops 8999999488 | bytes 83886080 | tf_op jit(solution)/shard_map/gather_proteins/pallas_call | solution.py:306
  55.6 0.0 collective-permute-done.1.got.refs_0_
  55.6 0.6 choose.1.chosen
  56.2 0.0 collective-permute-done.perm
  56.2 0.0 copy-start.1
  56.2 23.8 %cis.1 = (f32[4,256]{1,0:T(4,128)S(1)}, f32[2,8,184,128]{3,2,1,0:T(8,128)S(1)}) custom-call(s32[64]{0:T(128)S(1)} %get-tuple-element.10.plan, s32[4,1024]{1,0:T(4,128)S(1)} %collective-permute-done.perm, bf16[8,184,2048]{2,1,0:T(8,128)(2,1)S(1)} %bitcast.6, bf16[512,1024]{1,0:T(8,128)(2,1)S(1)} %get-tuple-element.11.chosen.chosen_own, ...), custom_call_target="tpu_custom_call" | custom-call | flops 12000000000 | bytes 20971520 | tf_op jit(solution)/shard_map/cis/pallas_call | solution.py:433
  80.0 0.6 slice_multiply_fusion
  80.6 0.0 collective-permute-done.2.refs_1_
  80.6 0.0 copy-done.1
  80.6 14.3 %trans.1 = bf16[1472,1536]{1,0:T(8,128)(2,1)} custom-call(s32[64]{0:T(128)S(1)} %get-tuple-element.10.plan, bf16[1472,2048]{1,0:T(8,128)(2,1)S(1)} %bitcast.7, f32[2,1472,128]{2,1,0:T(8,128)S(1)} %bitcast.8, bf16[1536,1024]{1,0:T(8,128)(2,1)S(1)} %copy-done.1, bf16[512,1024]{1,0:T(8,128)(2,1)S(1)} %collective-permute-done.1.got.refs_0_, ...), custom_call_target="tpu_custom_call" | custom-call | flops 9261023232 | bytes 8388608 | tf_op jit(solution)/shard_map/trans/pallas_call | solution.py:508
Async XLA Ops:
  0.6 1.9 %copy-start = (bf16[1536,1024]{1,0:T(8,128)(2,1)S(1)}, bf16[1536,1024]{1,0:T(8,128)(2,1)}, u32[]{:S(2)}) copy-start(bf16[1536,1024]{1,0:T(8,128)(2,1)} %g_ref.3) | copy-start | bytes 9437188
  2.5 0.7 copy-start.2
  3.2 3.8 %copy-start.4 = (s32[4,1024]{1,0:T(4,128)S(1)}, s32[4,1024]{1,0:T(4,128)}, u32[]{:S(2)}) copy-start(s32[4,1024]{1,0:T(4,128)} %perm.1) | copy-start | bytes 49156
  3.2 5.3 %copy-start.3 = (bf16[1024,184]{0,1:T(8,128)(2,1)S(1)}, bf16[1024,184]{0,1:T(8,128)(2,1)}, u32[]{:S(2)}) copy-start(bf16[1024,184]{0,1:T(8,128)(2,1)} %param.5) | copy-start | bytes 1130500
  4.8 50.7 %collective-permute-start.1 = (bf16[512,1024]{1,0:T(8,128)(2,1)S(1)}, bf16[512,1024]{1,0:T(8,128)(2,1)S(1)}, u32[]{:S(2)}, u32[]{:S(2)}) collective-permute-start(bf16[512,1024]{1,0:T(8,128)(2,1)S(1)} %get-tuple-element.13), channel_id=1, source_target_pairs={{0,1},{1,0},{2,3},{3,2},{4,5},{5,4},{6,7},{7,6},{8,9},{9,8},{10,11... | collective-permute-start | bytes 3145736 | tf_op jit(solution)/shard_map/ppermute | solution.py:534
  7.0 49.2 %collective-permute-start = (s32[4,1024]{1,0:T(4,128)S(1)}, s32[4,1024]{1,0:T(4,128)S(1)}, u32[]{:S(2)}, u32[]{:S(2)}) collective-permute-start(s32[4,1024]{1,0:T(4,128)S(1)} %copy-done.4), channel_id=1, source_target_pairs={{0,1},{1,0},{2,3},{3,2},{4,5},{5,4},{6,7},{7,6},{8,9},{9,8},{10,11... | collective-permute-start | bytes 49160 | tf_op jit(solution)/shard_map/ppermute | solution.py:532
  7.1 73.5 %collective-permute-start.2 = (bf16[1024,1024]{1,0:T(8,128)(2,1)S(1)}, bf16[1024,1024]{1,0:T(8,128)(2,1)S(1)}, u32[]{:S(2)}, u32[]{:S(2)}) collective-permute-start(bf16[1024,1024]{1,0:T(8,128)(2,1)S(1)} %get-tuple-element.16), channel_id=1, source_target_pairs={{0,1},{1,0},{2,3},{3,2},{4,5},{5,4},{6,7},{7,6},{8,9},{9,8},{10,11... | collective-permute-start | bytes 6291464 | tf_op jit(solution)/shard_map/ppermute | solution.py:534
  56.2 24.4 %copy-start.1 = (bf16[1536,1024]{1,0:T(8,128)(2,1)S(1)}, bf16[1536,1024]{1,0:T(8,128)(2,1)}, u32[]{:S(2)}) copy-start(bf16[1536,1024]{1,0:T(8,128)(2,1)} %g_ref.3) | copy-start | bytes 9437188
